TPU v7x, 32 devices: a whole 2x2x4 slice. The times are simulated.
32 devices in a mesh: ctx: 4 (over y, core), enc: 8 (over z, x).
Axes of the slice: x: 2, y: 2, z: 4, core: 2. Of those that a mesh axis runs over, the one named last changes fastest.
Arguments:
- queries: bfloat16 [8, 512, 4096], P('enc', 'ctx'), may hold values from -200 to 200
- d_out: bfloat16 [8, 512, 4096], P('enc', 'ctx'), may hold values from -24 to 24
- text_sample: int32 [8, 512], P('enc', 'ctx'), may hold values from 0 to 1, as said below
- tiles: int32 [8, 2], P('enc'), may hold values from 1 to 4
- img_k: bfloat16 [8, 512, 1024], P(None, ('ctx', 'enc')), may hold values from -20 to 20
- img_v: bfloat16 [8, 512, 1024], P(None, ('ctx', 'enc')), may hold values from -6 to 6
Outputs:
- d_queries: bfloat16 [8, 512, 4096], P('enc', 'ctx')
- d_img_k: bfloat16 [8, 512, 1024], P(None, ('ctx', 'enc'))
- d_img_v: bfloat16 [8, 512, 1024], P(None, ('ctx', 'enc'))
Inputs may be any that keep to these rules, and one draw needn't show every extreme that they name: `text_sample`: within each group the sample numbers never fall along the text, and each of the 2 samples has at least one token.
All inputs are finite; a program needn't handle non-finite values.
Results may differ from a plain program's by a relative error of at most 0.022.
Values may be sent and summed in bfloat16 or wider, within the bound.
No kernel may reach another device: no remote copies, remote signals or barrier semaphores. Data moves between devices by JAX's collectives and lax.ppermute only.
A program may use at most 128 MiB of HBM per device.

v0:
```python
import functools

import jax
import jax.numpy as jnp
from jax import lax
from jax.experimental import pallas as pl
from jax.experimental.pallas import tpu as pltpu
from jax.sharding import PartitionSpec as P

H = 32
KVH = 8
HD = 128
SAMP = 2
MAX_TILES = 4
TILE_TOK = 64
RATIO = H // KVH
CORES = 2
SLOT_ROWS = MAX_TILES * TILE_TOK
HALF_KV = KVH // CORES
HALF_KCOLS = HALF_KV * HD
HALF_QCOLS = HALF_KCOLS * RATIO
WIDE = RATIO * HD
CHUNKS = 2
CHUNK_KV = HALF_KV // CHUNKS
CHUNK_KCOLS = CHUNK_KV * HD
CHUNK_QCOLS = CHUNK_KV * WIDE
BLOCKS = 4
SAMP_ROWS = 16
SCALE = HD ** (-0.5)
LOG2E = 1.4426950408889634
BIG_NEGATIVE = -1e30
NT = (((1,), (1,)), ((), ()))
TN = (((0,), (0,)), ((), ()))
BF16 = jnp.bfloat16
F32 = jnp.float32

IN_VMEM = pl.BlockSpec(memory_space=pltpu.VMEM)
IN_HBM = pl.BlockSpec(memory_space=pltpu.HBM)


def local_call(body, ins, outs, scratch=(), flops=0, moved=2**19, aliases={}):
    return pl.pallas_call(
        body,
        in_specs=ins,
        out_specs=[spec for _, _, spec in outs],
        out_shape=[jax.ShapeDtypeStruct(s, d) for s, d, _ in outs],
        scratch_shapes=list(scratch),
        compiler_params=pltpu.CompilerParams(vmem_limit_bytes=8 * 2**20),
        input_output_aliases=aliases,
        cost_estimate=pl.CostEstimate(
            flops=flops, bytes_accessed=moved, transcendentals=flops // 1280
        ),
    )


def in_vmem(body, outs, **more):
    def call(*args):
        spec = [(shape, dtype, IN_VMEM) for shape, dtype in outs]
        return local_call(body, [IN_VMEM] * len(args), spec, **more)(*args)

    return call


def core_of():
    return lax.rem(lax.axis_index("ctx"), CORES)


def at_rows(first, count):
    return pl.ds(pl.multiple_of(first, count), count)


def at_cols(first, width, step):
    return pl.ds(pl.multiple_of(first, step), width)


def start_copies(pairs, sems):
    copies = [pltpu.make_async_copy(src, dst, sems.at[i]) for i, (src, dst) in enumerate(pairs)]
    for copy in copies:
        copy.start()
    return copies


def run_copies(pairs, sems):
    for copy in start_copies(pairs, sems):
        copy.wait()


def in_hbm(*arrays):
    return [pltpu.with_memory_space_constraint(a, pltpu.HBM) for a in arrays]


def carried(j, core):
    return BLOCKS * (1 - core) + j


def split_kernel(*refs):
    k_ref, v_ref, q_ref, g_ref, samp_hbm, tiles_hbm, mine, peer = refs[:8]
    text_refs, (samp, tiles, sems, small_sems) = refs[8:-4], refs[-4:]
    core = core_of()
    enc = lax.axis_index("enc")
    pairs = []
    for who, out in ((1 - core, peer), (core, mine)):
        for j in range(BLOCKS):
            for i, ref in enumerate((k_ref, v_ref)):
                pairs.append((ref.at[enc ^ carried(j, who)], out.at[i, j]))
    copies = start_copies(pairs, sems)
    split_text(
        2 * BLOCKS, CORES, near_place, q_ref, g_ref, samp_hbm, tiles_hbm, *text_refs, samp, tiles, small_sems
    )
    for copy in copies:
        copy.wait()


def near_place():
    y = lax.div(lax.axis_index("ctx"), CORES)
    return y, lax.axis_index("enc") ^ carried(0, core_of())


def split_text(n_blocks, pieces, where, q_ref, g_ref, samp_hbm, tiles_hbm, peer, q_own, g_own, bias, samp, tiles, sems):
    core = core_of()
    tokens = q_ref.shape[1]
    own_cols = at_cols(core * HALF_QCOLS, HALF_QCOLS, HALF_QCOLS)
    peer_cols = at_cols((1 - core) * HALF_QCOLS, HALF_QCOLS, HALF_QCOLS)
    copies = start_copies(
        [
            (samp_hbm, samp),
            (tiles_hbm, tiles),
            (q_ref.at[0, :, peer_cols], peer.at[:tokens]),
            (g_ref.at[0, :, peer_cols], peer.at[tokens : 2 * tokens]),
            (q_ref.at[0, :, own_cols], q_own.at[:tokens]),
            (g_ref.at[0, :, own_cols], g_own),
        ],
        sems,
    )
    for copy in copies[:2]:
        copy.wait()
    row = jnp.broadcast_to(samp[...].astype(F32), (SAMP_ROWS, tokens)).astype(BF16)
    for out, first in ((q_own, tokens), (peer, 2 * tokens)):
        out[first:, :] = jnp.zeros((SAMP_ROWS, HALF_QCOLS), BF16)
        out[first:, :tokens] = row

    sample, offset = where()
    block_rows = SLOT_ROWS // n_blocks
    slots = block_rows // pieces
    line = lax.broadcasted_iota(jnp.int32, (SLOT_ROWS, HD), 0)
    owner = lax.div(line, block_rows) ^ offset
    piece = lax.rem(lax.div(line, slots), pieces)
    slot = piece * (SLOT_ROWS // pieces) + owner * slots + lax.rem(line, slots)
    for i in range(SAMP):
        count = jnp.where((sample ^ i) == 0, tiles[0:1, 0:1], tiles[0:1, 1:2])
        bias[i] = jnp.where(slot < count * TILE_TOK, 0.0, BIG_NEGATIVE)
    for copy in copies[2:]:
        copy.wait()


def carry_kernel(slots, mine, got, text, *outs):
    core = core_of()
    for j, out in enumerate(outs[:-1]):
        for i in range(2):
            first = i * CORES * slots
            out[at_rows(first + core * slots, slots), :] = mine[i, j]
            out[at_rows(first + (1 - core) * slots, slots), :] = got[i, j]


def join_kernel(*refs):
    parts, out = refs[:-1], refs[-1]
    rows = parts[0].shape[0]
    for i, part in enumerate(parts):
        out[i * rows : (i + 1) * rows, :] = part[...]


def split_cols_kernel(*refs):
    parts, out = refs[: BLOCKS // 2], refs[-1]
    rows = parts[0].shape[0]
    cols = at_cols((1 - core_of()) * HALF_KCOLS, HALF_KCOLS, HALF_KCOLS)
    for i, part in enumerate(parts):
        out[i * rows : (i + 1) * rows, :] = part[:, cols]


def add_kernel(*refs):
    own, back, outs = refs[:CHUNKS], refs[CHUNKS : 2 * CHUNKS], refs[2 * CHUNKS :]
    rows = outs[0].shape[0]
    for i, out in enumerate(outs):
        part = slice(i * rows, (i + 1) * rows)
        for c in range(CHUNKS):
            cols = slice(c * CHUNK_KCOLS, (c + 1) * CHUNK_KCOLS)
            out[:, cols] = (own[c][part, :] + back[c][part, :].astype(F32)).astype(out.dtype)


def back_kernel(mine, got, *outs):
    core = core_of()
    rows = outs[0].shape[0]
    own_cols = at_cols(core * HALF_KCOLS, HALF_KCOLS, HALF_KCOLS)
    got_cols = at_cols((1 - core) * HALF_KCOLS, HALF_KCOLS, HALF_KCOLS)
    for j, out in enumerate(outs):
        out[:, own_cols] = mine[j * rows : (j + 1) * rows, :]
        out[:, got_cols] = got[j * rows : (j + 1) * rows, :]


def owner_rows_kernel(slots, *refs):
    blocks, (mine, peer) = refs[: BLOCKS], refs[-2:]
    core = core_of()
    for j, block in enumerate(blocks):
        for i in range(2):
            first = i * CORES * slots
            mine[i, j] = block[at_rows(first + core * slots, slots), :]
            peer[i, j] = block[at_rows(first + (1 - core) * slots, slots), :]


def finish_kernel(mine, got, dk, dv, sems):
    core = core_of()
    enc = lax.axis_index("enc")
    pairs = []
    for who, ref in ((core, mine), (1 - core, got)):
        for j in range(BLOCKS):
            for i, out in enumerate((dk, dv)):
                pairs.append((ref.at[i, j], out.at[enc ^ carried(j, who)]))
    run_copies(pairs, sems)


def finish_text_kernel(*refs):
    refs, (out, token, sems) = refs[:-3], refs[-3:]
    core = core_of()
    token[...] = jnp.zeros_like(token)
    pairs = []
    for c in range(CHUNKS):
        for half, ref in ((core, refs[2 * c]), (1 - core, refs[2 * c + 1])):
            cols = at_cols(half * HALF_QCOLS + c * CHUNK_QCOLS, CHUNK_QCOLS, CHUNK_QCOLS)
            pairs.append((ref, out.at[0, :, cols]))
    run_copies(pairs, sems)


def pass_kernel(role, chunk, n_blocks, n_kv, with_prev, where, bias, q_a, g_a, got, *rest):
    kvs, rest = rest[:n_kv], rest[n_kv:]
    prev = None
    if with_prev:
        prev, rest = rest[:2], rest[2:]
    *dqs, grads = rest
    sample = where()[0] ^ role
    tokens = g_a.shape[0]
    block_rows = SLOT_ROWS // n_blocks
    row_a = q_a[tokens : tokens + 1, :tokens].astype(F32)
    row_b = got[2 * tokens : 2 * tokens + 1, :tokens].astype(F32)
    wanted = sample.astype(F32)
    has = jnp.where(row_a == wanted, 1.0, jnp.where(row_b == wanted, 1.0, 0.0))
    present = jnp.max(has) > 0.5

    @pl.when(present)
    def _():
        mine = jnp.concatenate([row_a] * RATIO + [row_b] * RATIO, axis=1) == wanted
        for h in range(CHUNK_KV):
            first_q = chunk * CHUNK_QCOLS + h * WIDE
            first_k = chunk * CHUNK_KCOLS + h * HD

            def stacked(ref_a, first_b):
                parts = [
                    ref[first : first + tokens, first_q + r * HD : first_q + (r + 1) * HD]
                    for ref, first in ((ref_a, 0), (got, first_b))
                    for r in range(RATIO)
                ]
                return jnp.concatenate(parts, axis=0)

            def rows_of(first):
                parts = []
                for kv in kvs:
                    if kv.shape[1] == HALF_KCOLS:
                        cols = slice(first_k, first_k + HD)
                    else:
                        cols = at_cols(core_of() * HALF_KCOLS + first_k, HD, HD)
                    for at in range(first, kv.shape[0], 2 * block_rows):
                        parts.append(kv[at : at + block_rows, cols])
                return jnp.concatenate(parts, axis=0)

            q = stacked(q_a, 0)
            g = stacked(g_a, tokens)
            k = rows_of(0)
            v = rows_of(block_rows)
            s = lax.dot_general(k, q, NT, preferred_element_type=F32)
            s = s + jnp.concatenate([bias[role]] * (s.shape[1] // HD), axis=1)
            top = jnp.max(s, axis=0, keepdims=True)
            e = jnp.exp2((s - top) * (SCALE * LOG2E))
            total = jnp.sum(e, axis=0, keepdims=True)
            p = e * jnp.where(mine, 1.0 / total, 0.0)
            gp = lax.dot_general(v, g, NT, preferred_element_type=F32)
            row_dot = jnp.sum(p * gp, axis=0, keepdims=True)
            ds = (p * (gp - row_dot)).astype(BF16)
            dv = jnp.dot(p.astype(BF16), g, preferred_element_type=F32)
            dk = jnp.dot(ds, q, preferred_element_type=F32) * SCALE
            dq = lax.dot_general(ds, k, TN, preferred_element_type=F32) * SCALE
            for t, dq_ref in enumerate(dqs):
                for r in range(RATIO):
                    at = (t * RATIO + r) * tokens
                    cols = slice(h * WIDE + r * HD, h * WIDE + (r + 1) * HD)
                    part = dq[at : at + tokens]
                    if with_prev:
                        part = part + prev[t][:, cols].astype(F32)
                    dq_ref[:, cols] = part.astype(dq_ref.dtype)
            cols = slice(h * HD, (h + 1) * HD)
            for b in range(n_blocks):
                rows = slice(b * block_rows, (b + 1) * block_rows)
                first = b * 2 * block_rows
                grads[first : first + block_rows, cols] = dk[rows].astype(grads.dtype)
                grads[first + block_rows : first + 2 * block_rows, cols] = dv[rows].astype(grads.dtype)

    @pl.when(jnp.logical_not(present))
    def _():
        grads[...] = jnp.zeros_like(grads)
        for t, dq_ref in enumerate(dqs):
            dq_ref[...] = prev[t][...] if with_prev else jnp.zeros_like(dq_ref)


def sample_pass(where, role, chunk, n_blocks, bias, text, kvs, prev, grad_dtype):
    tokens = text[1].shape[0]
    dq = ((tokens, CHUNK_QCOLS), BF16)
    pairs = tokens * WIDE * SLOT_ROWS * CORES * CHUNK_KV
    dq_a, dq_b, grads = in_vmem(
        functools.partial(
            pass_kernel, role, chunk, n_blocks, len(kvs), prev is not None, where
        ),
        [dq, dq, ((2 * SLOT_ROWS, CHUNK_KCOLS), grad_dtype)],
        flops=10 * pairs,
        moved=8 * 2**20,
    )(bias, *text, *kvs, *(prev or ()))
    return (dq_a, dq_b), grads


def shards(n_ctx, n_enc, queries, d_out, text_sample, tiles, img_k, img_v):
    n_y = n_ctx // CORES
    slots = img_k.shape[1]
    tokens = queries.shape[1]
    swap_core = [(i, i ^ 1) for i in range(n_ctx)]
    near = n_y == SAMP and slots % 16 == 0 and n_enc == 2 * BLOCKS
    dqs = [None] * CHUNKS
    text_outs = [
        ((2 * tokens + SAMP_ROWS, HALF_QCOLS), BF16, IN_VMEM),
        ((tokens + SAMP_ROWS, HALF_QCOLS), BF16, IN_VMEM),
        ((tokens, HALF_QCOLS), BF16, IN_VMEM),
        ((SAMP, SLOT_ROWS, HD), F32, IN_VMEM),
    ]
    text_scratch = [
        pltpu.VMEM(text_sample.shape, jnp.int32),
        pltpu.VMEM(tiles.shape, jnp.int32),
    ]
    text_sems = pltpu.SemaphoreType.DMA((6,))

    if near:
        swap_y = [(i, (i + CORES) % n_ctx) for i in range(n_ctx)]
        block = (2 * CORES * slots, KVH * HD)
        pair = (2 * block[0], block[1])
        half = (BLOCKS * block[0], HALF_KCOLS)
        slabs = (2, BLOCKS, slots, KVH * HD)

        def around(parts):
            return [
                lax.ppermute(
                    part,
                    ("ctx", "enc"),
                    [
                        (i * n_enc + e, i * n_enc + (e ^ carried(j, i % CORES)))
                        for i in range(n_ctx)
                        for e in range(n_enc)
                    ],
                )
                for j, part in enumerate(parts)
            ]

        mine, for_peer, text_peer, q_own, g_own, bias = local_call(
            split_kernel,
            [IN_HBM] * 6,
            [(slabs, BF16, IN_VMEM)] * 2 + text_outs,
            text_scratch + [pltpu.SemaphoreType.DMA((4 * BLOCKS,)), text_sems],
            moved=4 * 2**20,
        )(*in_hbm(img_k, img_v, queries, d_out, text_sample, tiles))
        *carry, text_peer = in_vmem(
            functools.partial(carry_kernel, slots),
            [(block, BF16)] * BLOCKS + [(text_peer.shape, BF16)],
            aliases={2: BLOCKS},
        )(mine, lax.ppermute(for_peer, "ctx", swap_core), text_peer)
        text = (q_own, g_own, lax.ppermute(text_peer, "ctx", swap_core))
        brought = around(carry)

        def with_other_core(parts, after=()):
            (for_peer,) = in_vmem(split_cols_kernel, [(half, BF16)])(*parts, *after)
            return [*parts, lax.ppermute(for_peer, "ctx", swap_core)]

        own, far = [], []
        for j in range(0, BLOCKS, 2):
            own += in_vmem(join_kernel, [(pair, BF16)])(*brought[j : j + 2])
            far.append(lax.ppermute(own[-1], "ctx", swap_y))
        own = with_other_core(own)

        own_grads, back = [None] * CHUNKS, [None] * CHUNKS
        for c in range(CHUNKS):
            dqs[c], own_grads[c] = sample_pass(
                near_place, 0, c, n_enc, bias, text, own, None, F32
            )
        far = with_other_core(far, [pair[0] for pair in dqs])
        for c in range(CHUNKS):
            dqs[c], grads = sample_pass(
                near_place, 1, c, n_enc, bias, text, far, dqs[c], BF16
            )
            back[c] = lax.ppermute(grads, "ctx", swap_y)
        mine, for_peer = in_vmem(add_kernel, [(half, BF16)] * 2)(*own_grads, *back)
        carry = in_vmem(back_kernel, [(block, BF16)] * BLOCKS)(
            mine, lax.ppermute(for_peer, "ctx", swap_core)
        )
        brought = around(carry)
    else:
        both = ("ctx", "enc")
        same_y = [
            [yy * CORES * n_enc + i for i in range(CORES * n_enc)] for yy in range(n_y)
        ]
        same_column = [
            [(yy * CORES + c) * n_enc + e for yy in range(n_y)]
            for c in range(CORES)
            for e in range(n_enc)
        ]
        core = core_of()

        def exchange(parts):
            return lax.all_to_all(
                parts, both, split_axis=0, concat_axis=0, axis_index_groups=same_y, tiled=True
            )

        def to_groups(owned):
            parts = owned.reshape(n_enc, slots, CORES, HALF_KCOLS).transpose(2, 0, 1, 3)
            got = exchange(parts.reshape(CORES * n_enc, slots, HALF_KCOLS))
            got = got.reshape(CORES * n_enc * slots, HALF_KCOLS)
            return lax.all_gather(got, both, axis=0, axis_index_groups=same_column, tiled=True)

        def to_owners(grads):
            grads = lax.psum_scatter(
                grads, both, scatter_dimension=0, axis_index_groups=same_column, tiled=True
            )
            got = exchange(grads.reshape(CORES * n_enc, slots, HALF_KCOLS))
            got = got.reshape(CORES, n_enc, slots, HALF_KCOLS).transpose(1, 2, 0, 3)
            return got.reshape(n_enc, slots, CORES * HALF_KCOLS)

        def no_place():
            return jnp.int32(0), jnp.int32(0)

        all_k = to_groups(img_k)
        all_v = to_groups(img_v)
        text_peer, q_own, g_own, bias = local_call(
            functools.partial(split_text, 1, 1, no_place),
            [IN_HBM] * 4,
            text_outs,
            text_scratch + [text_sems],
            moved=4 * 2**20,
        )(*in_hbm(queries, d_out, text_sample, tiles))
        text = (q_own, g_own, lax.ppermute(text_peer, "ctx", swap_core))
        dks = [[None] * CHUNKS for _ in range(SAMP)]
        dvs = [[None] * CHUNKS for _ in range(SAMP)]
        for sample in range(SAMP):
            rows = slice(sample * SLOT_ROWS, (sample + 1) * SLOT_ROWS)
            kv = jnp.concatenate([all_k[rows], all_v[rows]], axis=0)
            for c in range(CHUNKS):
                dqs[c], grads = sample_pass(no_place, sample, c, 1, bias, text, [kv], dqs[c], BF16)
                dks[sample][c] = grads[:SLOT_ROWS]
                dvs[sample][c] = grads[SLOT_ROWS:]
        d_img_k = to_owners(jnp.block(dks))
        d_img_v = to_owners(jnp.block(dvs))

    ends = []
    for c in range(CHUNKS):
        ends += [dqs[c][0], lax.ppermute(dqs[c][1], "ctx", swap_core)]
    d_queries, token = local_call(
        finish_text_kernel,
        [IN_VMEM] * len(ends),
        [(queries.shape, BF16, IN_HBM), ((8, HD), F32, IN_VMEM)],
        [pltpu.SemaphoreType.DMA((2 * CHUNKS,))],
    )(*ends)
    if near:
        mine, for_peer = in_vmem(
            functools.partial(owner_rows_kernel, slots), [(slabs, BF16)] * 2
        )(*brought, token)
        d_img_k, d_img_v = local_call(
            finish_kernel,
            [IN_VMEM] * 2,
            [(img_k.shape, BF16, IN_HBM)] * 2,
            [pltpu.SemaphoreType.DMA((4 * BLOCKS,))],
        )(mine, lax.ppermute(for_peer, "ctx", swap_core))
    return (d_queries, d_img_k, d_img_v)


def solution(mesh):
    in_specs = (
        P("enc", "ctx", None),
        P("enc", "ctx", None),
        P("enc", "ctx"),
        P("enc", None),
        P(None, ("ctx", "enc"), None),
        P(None, ("ctx", "enc"), None),
    )
    out_specs = (
        P("enc", "ctx", None),
        P(None, ("ctx", "enc"), None),
        P(None, ("ctx", "enc"), None),
    )
    body = functools.partial(shards, mesh.shape["ctx"], mesh.shape["enc"])
    return jax.shard_map(body, mesh=mesh, in_specs=in_specs, out_specs=out_specs, check_vma=False)
```

profile of v0, /device:TPU:0, one launch (start us, length us, event | category | flops | bytes accessed | tf_op | source)
XLA Modules:
  0.0 76.9 jit_solution(867867636809516202)
XLA Ops:
  0.6 2.0 %shard_map.85 = (bf16[2,4,16,1024]{3,2,1,0:T(8,128)(2,1)S(1)}, bf16[2,4,16,1024]{3,2,1,0:T(8,128)(2,1)S(1)}, bf16[272,2048]{1,0:T(8,128)(2,1)S(1)}, bf16[144,204...) custom-call(bf16[8,16,1024]{2,1,0:T(8,128)(2,1)} %refs_0_.1, ...), custom_call_target="tpu_custom_call" | custom-call | bytes 4194304 | tf_op jit(solution)/shard_map/pallas_call | solution.py:367
  2.7 0.5 collective-permute-start
  3.2 1.2 %collective-permute-done.got = bf16[2,4,16,1024]{3,2,1,0:T(8,128)(2,1)S(1)} collective-permute-done((bf16[2,4,16,1024]{3,2,1,0:T(8,128)(2,1)S(1)}, bf16[2,4,16,1024]{3,2,1,0:T(8,128)(2,1)S(1)}, u32[]{:S(2)}, u32[]{:S(2)}) %collective-permute-start) | collective-permute-done | bytes 262176 | tf_op jit(solution)/shard_map/ppermute | solution.py:378
  4.4 0.4 collective-permute-start.1
  4.8 5.6 %collective-permute-start.2 = (bf16[64,1024]{1,0:T(8,128)(2,1)S(1)}, bf16[64,1024]{1,0:T(8,128)(2,1)S(1)}, u32[]{:S(2)}, u32[]{:S(2)}) collective-permute-start(bf16[64,1024]{1,0:T(8,128)(2,1)S(1)} %get-tuple-element.45), channel_id=1, source_target_pairs={{0,4},{1,5},{2,6},{3,7},{4,0},{5,1},{6,2},{7,3},{8,8},{9,9},{10,10... | collective-permute-start | bytes 393224 | tf_op jit(solution)/shard_map/ppermute | solution.py:355
  10.5 1.3 %collective-permute-start.3 = (bf16[64,1024]{1,0:T(8,128)(2,1)S(1)}, bf16[64,1024]{1,0:T(8,128)(2,1)S(1)}, u32[]{:S(2)}, u32[]{:S(2)}) collective-permute-start(bf16[64,1024]{1,0:T(8,128)(2,1)S(1)} %get-tuple-element.46), channel_id=1, source_target_pairs={{0,5},{1,4},{2,7},{3,6},{4,1},{5,0},{6,3},{7,2},{8,9},{9,8},{10,11... | collective-permute-start | bytes 393224 | tf_op jit(solution)/shard_map/ppermute | solution.py:355
  11.8 3.6 %collective-permute-start.5 = (bf16[64,1024]{1,0:T(8,128)(2,1)S(1)}, bf16[64,1024]{1,0:T(8,128)(2,1)S(1)}, u32[]{:S(2)}, u32[]{:S(2)}) collective-permute-start(bf16[64,1024]{1,0:T(8,128)(2,1)S(1)} %get-tuple-element.47), channel_id=1, source_target_pairs={{0,6},{1,7},{2,4},{3,5},{4,2},{5,3},{6,0},{7,1},{8,10},{9,11},{10,... | collective-permute-start | bytes 393224 | tf_op jit(solution)/shard_map/ppermute | solution.py:355
  15.4 0.0 collective-permute-start.6
  15.4 0.0 collective-permute-done.2.refs_0_
  15.4 4.9 %collective-permute-done.3.refs_1_ = bf16[64,1024]{1,0:T(8,128)(2,1)S(1)} collective-permute-done((bf16[64,1024]{1,0:T(8,128)(2,1)S(1)}, bf16[64,1024]{1,0:T(8,128)(2,1)S(1)}, u32[]{:S(2)}, u32[]{:S(2)}) %collective-permute-start.3) | collective-permute-done | bytes 131104 | tf_op jit(solution)/shard_map/ppermute | solution.py:355
  20.3 0.0 collective-permute-done.5.refs_0_
  20.4 2.8 %collective-permute-done.6.refs_1_ = bf16[64,1024]{1,0:T(8,128)(2,1)S(1)} collective-permute-done((bf16[64,1024]{1,0:T(8,128)(2,1)S(1)}, bf16[64,1024]{1,0:T(8,128)(2,1)S(1)}, u32[]{:S(2)}, u32[]{:S(2)}) %collective-permute-start.6) | collective-permute-done | bytes 131104 | tf_op jit(solution)/shard_map/ppermute | solution.py:355
  23.2 0.1 collective-permute-start.8
  23.3 1.6 %collective-permute-start.7 = (bf16[128,1024]{1,0:T(8,128)(2,1)S(1)}, bf16[128,1024]{1,0:T(8,128)(2,1)S(1)}, u32[]{:S(2)}, u32[]{:S(2)}) collective-permute-start(bf16[128,1024]{1,0:T(8,128)(2,1)S(1)} %shard_map.88.refs_1_.rest_1_), channel_id=1, source_target_pairs={{0,16},{8,24},{16,0},{24,8},{1,17},{9,25},{17,1},{25,9},{2,18},{10... | collective-permute-start | bytes 786440 | tf_op jit(solution)/shard_map/ppermute | solution.py:389
  24.9 0.5 collective-permute-start.4
  25.4 0.0 collective-permute-done.8.rest_2_
  25.4 0.0 collective-permute-done.1.got
  25.4 2.4 %shard_map.91 = (bf16[128,1024]{1,0:T(8,128)(2,1)S(1)}, bf16[128,1024]{1,0:T(8,128)(2,1)S(1)}, f32[512,256]{1,0:T(8,128)S(1)}) custom-call(f32[2,256,128]{2,1,0:T(8,128)S(1)} %get-tuple-element.38.bias, bf16[144,2048]{1,0:T(8,128)(2,1)S(1)} %get-tuple-element.39.q_a, bf16[128,2048]{1,0:T(8,128)(2,1)S(1)} %get-tuple-element.40.g_a, ...), custom_call_target="tpu_custom_call" | custom-call | flops 671088640 | bytes 8388608 | tf_op jit(solution)/shard_map/pallas_call | solution.py:59
  27.9 2.5 %shard_map.90 = (bf16[128,1024]{1,0:T(8,128)(2,1)S(1)}, bf16[128,1024]{1,0:T(8,128)(2,1)S(1)}, f32[512,256]{1,0:T(8,128)S(1)}) custom-call(f32[2,256,128]{2,1,0:T(8,128)S(1)} %get-tuple-element.38.bias, bf16[144,2048]{1,0:T(8,128)(2,1)S(1)} %get-tuple-element.39.q_a, bf16[128,2048]{1,0:T(8,128)(2,1)S(1)} %get-tuple-element.40.g_a, ...), custom_call_target="tpu_custom_call" | custom-call | flops 671088640 | bytes 8388608 | tf_op jit(solution)/shard_map/pallas_call | solution.py:59
  30.3 2.2 %collective-permute-done.7.refs_1_.rest_1_ = bf16[128,1024]{1,0:T(8,128)(2,1)S(1)} collective-permute-done((bf16[128,1024]{1,0:T(8,128)(2,1)S(1)}, bf16[128,1024]{1,0:T(8,128)(2,1)S(1)}, u32[]{:S(2)}, u32[]{:S(2)}) %collective-permute-start.7) | collective-permute-done | bytes 262176 | tf_op jit(solution)/shard_map/ppermute | solution.py:389
  32.5 5.2 %collective-permute-done.4.refs_0_.rest_0_ = bf16[128,1024]{1,0:T(8,128)(2,1)S(1)} collective-permute-done((bf16[128,1024]{1,0:T(8,128)(2,1)S(1)}, bf16[128,1024]{1,0:T(8,128)(2,1)S(1)}, u32[]{:S(2)}, u32[]{:S(2)}) %collective-permute-start.4) | collective-permute-done | bytes 262176 | tf_op jit(solution)/shard_map/ppermute | solution.py:389
  37.7 0.1 collective-permute-start.9
  37.8 1.5 %collective-permute-done.9.rest_2_ = bf16[256,512]{1,0:T(8,128)(2,1)S(1)} collective-permute-done((bf16[256,512]{1,0:T(8,128)(2,1)S(1)}, bf16[256,512]{1,0:T(8,128)(2,1)S(1)}, u32[]{:S(2)}, u32[]{:S(2)}) %collective-permute-start.9) | collective-permute-done | bytes 262176 | tf_op jit(solution)/shard_map/ppermute | solution.py:384
  39.3 2.4 %shard_map.94 = (bf16[128,1024]{1,0:T(8,128)(2,1)S(1)}, bf16[128,1024]{1,0:T(8,128)(2,1)S(1)}, bf16[512,256]{1,0:T(8,128)(2,1)S(1)}) custom-call(f32[2,256,128]{2,1,0:T(8,128)S(1)} %get-tuple-element.38.bias, bf16[144,2048]{1,0:T(8,128)(2,1)S(1)} %get-tuple-element.39.q_a, bf16[128,2048]{1,0:T(8,128)(2,1)S(1)} %get-tuple-element.40.g_a, ...), custom_call_target="tpu_custom_call" | custom-call | flops 671088640 | bytes 8388608 | tf_op jit(solution)/shard_map/pallas_call | solution.py:59
  41.7 0.1 collective-permute-start.13
  41.8 2.4 %shard_map.93 = (bf16[128,1024]{1,0:T(8,128)(2,1)S(1)}, bf16[128,1024]{1,0:T(8,128)(2,1)S(1)}, bf16[512,256]{1,0:T(8,128)(2,1)S(1)}) custom-call(f32[2,256,128]{2,1,0:T(8,128)S(1)} %get-tuple-element.38.bias, bf16[144,2048]{1,0:T(8,128)(2,1)S(1)} %get-tuple-element.39.q_a, bf16[128,2048]{1,0:T(8,128)(2,1)S(1)} %get-tuple-element.40.g_a, ...), custom_call_target="tpu_custom_call" | custom-call | flops 671088640 | bytes 8388608 | tf_op jit(solution)/shard_map/pallas_call | solution.py:59
  44.2 0.1 collective-permute-start.12
  44.3 6.6 %collective-permute-done.13.refs_3_ = bf16[512,256]{1,0:T(8,128)(2,1)S(1)} collective-permute-done((bf16[512,256]{1,0:T(8,128)(2,1)S(1)}, bf16[512,256]{1,0:T(8,128)(2,1)S(1)}, u32[]{:S(2)}, u32[]{:S(2)}) %collective-permute-start.13) | collective-permute-done | bytes 262176 | tf_op jit(solution)/shard_map/ppermute | solution.py:402
  50.9 4.8 %collective-permute-done.12.refs_2_ = bf16[512,256]{1,0:T(8,128)(2,1)S(1)} collective-permute-done((bf16[512,256]{1,0:T(8,128)(2,1)S(1)}, bf16[512,256]{1,0:T(8,128)(2,1)S(1)}, u32[]{:S(2)}, u32[]{:S(2)}) %collective-permute-start.12) | collective-permute-done | bytes 262176 | tf_op jit(solution)/shard_map/ppermute | solution.py:402
  55.7 0.1 shard_map.96
  55.8 0.1 collective-permute-start.14
  55.9 0.5 collective-permute-start.11
  56.4 0.1 collective-permute-start.10
  56.5 0.9 %collective-permute-done.14.got = bf16[256,512]{1,0:T(8,128)(2,1)S(1)} collective-permute-done((bf16[256,512]{1,0:T(8,128)(2,1)S(1)}, bf16[256,512]{1,0:T(8,128)(2,1)S(1)}, u32[]{:S(2)}, u32[]{:S(2)}) %collective-permute-start.14) | collective-permute-done | bytes 262176 | tf_op jit(solution)/shard_map/ppermute | solution.py:405
  57.5 5.7 %collective-permute-start.15 = (bf16[64,1024]{1,0:T(8,128)(2,1)S(1)}, bf16[64,1024]{1,0:T(8,128)(2,1)S(1)}, u32[]{:S(2)}, u32[]{:S(2)}) collective-permute-start(bf16[64,1024]{1,0:T(8,128)(2,1)S(1)} %get-tuple-element.64), channel_id=1, source_target_pairs={{0,4},{1,5},{2,6},{3,7},{4,0},{5,1},{6,2},{7,3},{8,8},{9,9},{10,10... | collective-permute-start | bytes 393224 | tf_op jit(solution)/shard_map/ppermute | solution.py:355
  63.2 0.3 collective-permute-start.16
  63.5 1.1 %collective-permute-start.17 = (bf16[64,1024]{1,0:T(8,128)(2,1)S(1)}, bf16[64,1024]{1,0:T(8,128)(2,1)S(1)}, u32[]{:S(2)}, u32[]{:S(2)}) collective-permute-start(bf16[64,1024]{1,0:T(8,128)(2,1)S(1)} %get-tuple-element.66), channel_id=1, source_target_pairs={{0,6},{1,7},{2,4},{3,5},{4,2},{5,3},{6,0},{7,1},{8,10},{9,11},{10,... | collective-permute-start | bytes 393224 | tf_op jit(solution)/shard_map/ppermute | solution.py:355
  64.6 0.0 collective-permute-done.11.refs_3_
  64.6 3.4 %collective-permute-start.18 = (bf16[64,1024]{1,0:T(8,128)(2,1)S(1)}, bf16[64,1024]{1,0:T(8,128)(2,1)S(1)}, u32[]{:S(2)}, u32[]{:S(2)}) collective-permute-start(bf16[64,1024]{1,0:T(8,128)(2,1)S(1)} %get-tuple-element.67), channel_id=1, source_target_pairs={{0,7},{1,6},{2,5},{3,4},{4,3},{5,2},{6,1},{7,0},{8,11},{9,10},{10,... | collective-permute-start | bytes 393224 | tf_op jit(solution)/shard_map/ppermute | solution.py:355
  68.0 0.0 collective-permute-done.10.refs_1_
  68.0 1.0 %shard_map.95 = (bf16[1,128,4096]{2,1,0:T(8,128)(2,1)}, f32[8,128]{1,0:T(8,128)S(1)}) custom-call(bf16[128,1024]{1,0:T(8,128)(2,1)S(1)} %get-tuple-element.52.refs_0_, bf16[128,1024]{1,0:T(8,128)(2,1)S(1)} %collective-permute-done.10.refs_1_, bf16[128,1024]{1,0:T(8,128)(2,1)S(1)} %get-tuple-element.55.refs_2_, ...), custom_call_target="tpu_custom_call" | custom-call | bytes 524288 | tf_op jit(solution)/shard_map/pallas_call | solution.py:467
  69.0 0.0 collective-permute-done.15.refs_0_
  69.0 5.3 %collective-permute-done.16.refs_1_ = bf16[64,1024]{1,0:T(8,128)(2,1)S(1)} collective-permute-done((bf16[64,1024]{1,0:T(8,128)(2,1)S(1)}, bf16[64,1024]{1,0:T(8,128)(2,1)S(1)}, u32[]{:S(2)}, u32[]{:S(2)}) %collective-permute-start.16) | collective-permute-done | bytes 131104 | tf_op jit(solution)/shard_map/ppermute | solution.py:355
  74.3 0.0 collective-permute-done.17.refs_2_
  74.3 0.0 collective-permute-done.18.refs_3_
  74.3 0.1 collective-permute-start.19
  74.4 1.5 %collective-permute-done.19.got = bf16[2,4,16,1024]{3,2,1,0:T(8,128)(2,1)S(1)} collective-permute-done((bf16[2,4,16,1024]{3,2,1,0:T(8,128)(2,1)S(1)}, bf16[2,4,16,1024]{3,2,1,0:T(8,128)(2,1)S(1)}, u32[]{:S(2)}, u32[]{:S(2)}) %collective-permute-start.19) | collective-permute-done | bytes 262176 | tf_op jit(solution)/shard_map/ppermute | solution.py:482
  76.0 0.9 %shard_map.99 = (bf16[8,16,1024]{2,1,0:T(8,128)(2,1)}, bf16[8,16,1024]{2,1,0:T(8,128)(2,1)}) custom-call(bf16[2,4,16,1024]{3,2,1,0:T(8,128)(2,1)S(1)} %get-tuple-element.69.mine, bf16[2,4,16,1024]{3,2,1,0:T(8,128)(2,1)S(1)} %collective-permute-done.19.got), custom_call_target="tpu_custom_call" | custom-call | bytes 524288 | tf_op jit(solution)/shard_map/pallas_call | solution.py:477
  (7 shorter events, 0.2 us)
Async XLA Ops:
  2.7 1.7 %collective-permute-start = (bf16[2,4,16,1024]{3,2,1,0:T(8,128)(2,1)S(1)}, bf16[2,4,16,1024]{3,2,1,0:T(8,128)(2,1)S(1)}, u32[]{:S(2)}, u32[]{:S(2)}) collective-permute-start(bf16[2,4,16,1024]{3,2,1,0:T(8,128)(2,1)S(1)} %get-tuple-element.42), channel_id=1, source_target_pairs={{0,8},{8,0},{16,24},{24,16},{1,9},{9,1},{17,25},{25,17},{2,10},{10... | collective-permute-start | bytes 786440 | tf_op jit(solution)/shard_map/ppermute | solution.py:378
  4.4 21.0 %collective-permute-start.1 = (bf16[272,2048]{1,0:T(8,128)(2,1)S(1)}, bf16[272,2048]{1,0:T(8,128)(2,1)S(1)}, u32[]{:S(2)}, u32[]{:S(2)}) collective-permute-start(bf16[272,2048]{1,0:T(8,128)(2,1)S(1)} %get-tuple-element.44), channel_id=1, source_target_pairs={{0,8},{8,0},{16,24},{24,16},{1,9},{9,1},{17,25},{25,17},{2,10},{10... | collective-permute-start | bytes 3342344 | tf_op jit(solution)/shard_map/ppermute | solution.py:379
  4.8 10.6 %collective-permute-start.2 = (bf16[64,1024]{1,0:T(8,128)(2,1)S(1)}, bf16[64,1024]{1,0:T(8,128)(2,1)S(1)}, u32[]{:S(2)}, u32[]{:S(2)}) collective-permute-start(bf16[64,1024]{1,0:T(8,128)(2,1)S(1)} %get-tuple-element.45), channel_id=1, source_target_pairs={{0,4},{1,5},{2,6},{3,7},{4,0},{5,1},{6,2},{7,3},{8,8},{9,9},{10,10... | collective-permute-start | bytes 393224 | tf_op jit(solution)/shard_map/ppermute | solution.py:355
  10.5 9.8 %collective-permute-start.3 = (bf16[64,1024]{1,0:T(8,128)(2,1)S(1)}, bf16[64,1024]{1,0:T(8,128)(2,1)S(1)}, u32[]{:S(2)}, u32[]{:S(2)}) collective-permute-start(bf16[64,1024]{1,0:T(8,128)(2,1)S(1)} %get-tuple-element.46), channel_id=1, source_target_pairs={{0,5},{1,4},{2,7},{3,6},{4,1},{5,0},{6,3},{7,2},{8,9},{9,8},{10,11... | collective-permute-start | bytes 393224 | tf_op jit(solution)/shard_map/ppermute | solution.py:355
  11.8 8.5 %collective-permute-start.5 = (bf16[64,1024]{1,0:T(8,128)(2,1)S(1)}, bf16[64,1024]{1,0:T(8,128)(2,1)S(1)}, u32[]{:S(2)}, u32[]{:S(2)}) collective-permute-start(bf16[64,1024]{1,0:T(8,128)(2,1)S(1)} %get-tuple-element.47), channel_id=1, source_target_pairs={{0,6},{1,7},{2,4},{3,5},{4,2},{5,3},{6,0},{7,1},{8,10},{9,11},{10,... | collective-permute-start | bytes 393224 | tf_op jit(solution)/shard_map/ppermute | solution.py:355
  15.4 7.8 %collective-permute-start.6 = (bf16[64,1024]{1,0:T(8,128)(2,1)S(1)}, bf16[64,1024]{1,0:T(8,128)(2,1)S(1)}, u32[]{:S(2)}, u32[]{:S(2)}) collective-permute-start(bf16[64,1024]{1,0:T(8,128)(2,1)S(1)} %get-tuple-element.48), channel_id=1, source_target_pairs={{0,7},{1,6},{2,5},{3,4},{4,3},{5,2},{6,1},{7,0},{8,11},{9,10},{10,... | collective-permute-start | bytes 393224 | tf_op jit(solution)/shard_map/ppermute | solution.py:355
  23.2 2.2 %collective-permute-start.8 = (bf16[256,512]{1,0:T(8,128)(2,1)S(1)}, bf16[256,512]{1,0:T(8,128)(2,1)S(1)}, u32[]{:S(2)}, u32[]{:S(2)}) collective-permute-start(bf16[256,512]{1,0:T(8,128)(2,1)S(1)} %shard_map.89), channel_id=1, source_target_pairs={{0,8},{8,0},{16,24},{24,16},{1,9},{9,1},{17,25},{25,17},{2,10},{10... | collective-permute-start | bytes 786440 | tf_op jit(solution)/shard_map/ppermute | solution.py:384
  23.3 9.2 %collective-permute-start.7 = (bf16[128,1024]{1,0:T(8,128)(2,1)S(1)}, bf16[128,1024]{1,0:T(8,128)(2,1)S(1)}, u32[]{:S(2)}, u32[]{:S(2)}) collective-permute-start(bf16[128,1024]{1,0:T(8,128)(2,1)S(1)} %shard_map.88.refs_1_.rest_1_), channel_id=1, source_target_pairs={{0,16},{8,24},{16,0},{24,8},{1,17},{9,25},{17,1},{25,9},{2,18},{10... | collective-permute-start | bytes 786440 | tf_op jit(solution)/shard_map/ppermute | solution.py:389
  24.9 12.8 %collective-permute-start.4 = (bf16[128,1024]{1,0:T(8,128)(2,1)S(1)}, bf16[128,1024]{1,0:T(8,128)(2,1)S(1)}, u32[]{:S(2)}, u32[]{:S(2)}) collective-permute-start(bf16[128,1024]{1,0:T(8,128)(2,1)S(1)} %shard_map.87.refs_0_.rest_0_), channel_id=1, source_target_pairs={{0,16},{8,24},{16,0},{24,8},{1,17},{9,25},{17,1},{25,9},{2,18},{10... | collective-permute-start | bytes 786440 | tf_op jit(solution)/shard_map/ppermute | solution.py:389
  37.7 1.6 %collective-permute-start.9 = (bf16[256,512]{1,0:T(8,128)(2,1)S(1)}, bf16[256,512]{1,0:T(8,128)(2,1)S(1)}, u32[]{:S(2)}, u32[]{:S(2)}) collective-permute-start(bf16[256,512]{1,0:T(8,128)(2,1)S(1)} %shard_map.92), channel_id=1, source_target_pairs={{0,8},{8,0},{16,24},{24,16},{1,9},{9,1},{17,25},{25,17},{2,10},{10... | collective-permute-start | bytes 786440 | tf_op jit(solution)/shard_map/ppermute | solution.py:384
  41.7 9.2 %collective-permute-start.13 = (bf16[512,256]{1,0:T(8,128)(2,1)S(1)}, bf16[512,256]{1,0:T(8,128)(2,1)S(1)}, u32[]{:S(2)}, u32[]{:S(2)}) collective-permute-start(bf16[512,256]{1,0:T(8,128)(2,1)S(1)} %get-tuple-element.61), channel_id=1, source_target_pairs={{0,16},{8,24},{16,0},{24,8},{1,17},{9,25},{17,1},{25,9},{2,18},{10... | collective-permute-start | bytes 786440 | tf_op jit(solution)/shard_map/ppermute | solution.py:402
  44.2 11.5 %collective-permute-start.12 = (bf16[512,256]{1,0:T(8,128)(2,1)S(1)}, bf16[512,256]{1,0:T(8,128)(2,1)S(1)}, u32[]{:S(2)}, u32[]{:S(2)}) collective-permute-start(bf16[512,256]{1,0:T(8,128)(2,1)S(1)} %get-tuple-element.60), channel_id=1, source_target_pairs={{0,16},{8,24},{16,0},{24,8},{1,17},{9,25},{17,1},{25,9},{2,18},{10... | collective-permute-start | bytes 786440 | tf_op jit(solution)/shard_map/ppermute | solution.py:402
  55.8 1.6 %collective-permute-start.14 = (bf16[256,512]{1,0:T(8,128)(2,1)S(1)}, bf16[256,512]{1,0:T(8,128)(2,1)S(1)}, u32[]{:S(2)}, u32[]{:S(2)}) collective-permute-start(bf16[256,512]{1,0:T(8,128)(2,1)S(1)} %get-tuple-element.63), channel_id=1, source_target_pairs={{0,8},{8,0},{16,24},{24,16},{1,9},{9,1},{17,25},{25,17},{2,10},{10... | collective-permute-start | bytes 786440 | tf_op jit(solution)/shard_map/ppermute | solution.py:405
  55.9 8.7 %collective-permute-start.11 = (bf16[128,1024]{1,0:T(8,128)(2,1)S(1)}, bf16[128,1024]{1,0:T(8,128)(2,1)S(1)}, u32[]{:S(2)}, u32[]{:S(2)}) collective-permute-start(bf16[128,1024]{1,0:T(8,128)(2,1)S(1)} %get-tuple-element.56), channel_id=1, source_target_pairs={{0,8},{8,0},{16,24},{24,16},{1,9},{9,1},{17,25},{25,17},{2,10},{10... | collective-permute-start | bytes 786440 | tf_op jit(solution)/shard_map/ppermute | solution.py:466
  56.4 11.6 %collective-permute-start.10 = (bf16[128,1024]{1,0:T(8,128)(2,1)S(1)}, bf16[128,1024]{1,0:T(8,128)(2,1)S(1)}, u32[]{:S(2)}, u32[]{:S(2)}) collective-permute-start(bf16[128,1024]{1,0:T(8,128)(2,1)S(1)} %get-tuple-element.53), channel_id=1, source_target_pairs={{0,8},{8,0},{16,24},{24,16},{1,9},{9,1},{17,25},{25,17},{2,10},{10... | collective-permute-start | bytes 786440 | tf_op jit(solution)/shard_map/ppermute | solution.py:466
  57.5 11.5 %collective-permute-start.15 = (bf16[64,1024]{1,0:T(8,128)(2,1)S(1)}, bf16[64,1024]{1,0:T(8,128)(2,1)S(1)}, u32[]{:S(2)}, u32[]{:S(2)}) collective-permute-start(bf16[64,1024]{1,0:T(8,128)(2,1)S(1)} %get-tuple-element.64), channel_id=1, source_target_pairs={{0,4},{1,5},{2,6},{3,7},{4,0},{5,1},{6,2},{7,3},{8,8},{9,9},{10,10... | collective-permute-start | bytes 393224 | tf_op jit(solution)/shard_map/ppermute | solution.py:355
  63.2 11.1 %collective-permute-start.16 = (bf16[64,1024]{1,0:T(8,128)(2,1)S(1)}, bf16[64,1024]{1,0:T(8,128)(2,1)S(1)}, u32[]{:S(2)}, u32[]{:S(2)}) collective-permute-start(bf16[64,1024]{1,0:T(8,128)(2,1)S(1)} %get-tuple-element.65), channel_id=1, source_target_pairs={{0,5},{1,4},{2,7},{3,6},{4,1},{5,0},{6,3},{7,2},{8,9},{9,8},{10,11... | collective-permute-start | bytes 393224 | tf_op jit(solution)/shard_map/ppermute | solution.py:355
  63.5 10.9 %collective-permute-start.17 = (bf16[64,1024]{1,0:T(8,128)(2,1)S(1)}, bf16[64,1024]{1,0:T(8,128)(2,1)S(1)}, u32[]{:S(2)}, u32[]{:S(2)}) collective-permute-start(bf16[64,1024]{1,0:T(8,128)(2,1)S(1)} %get-tuple-element.66), channel_id=1, source_target_pairs={{0,6},{1,7},{2,4},{3,5},{4,2},{5,3},{6,0},{7,1},{8,10},{9,11},{10,... | collective-permute-start | bytes 393224 | tf_op jit(solution)/shard_map/ppermute | solution.py:355
  64.6 9.7 %collective-permute-start.18 = (bf16[64,1024]{1,0:T(8,128)(2,1)S(1)}, bf16[64,1024]{1,0:T(8,128)(2,1)S(1)}, u32[]{:S(2)}, u32[]{:S(2)}) collective-permute-start(bf16[64,1024]{1,0:T(8,128)(2,1)S(1)} %get-tuple-element.67), channel_id=1, source_target_pairs={{0,7},{1,6},{2,5},{3,4},{4,3},{5,2},{6,1},{7,0},{8,11},{9,10},{10,... | collective-permute-start | bytes 393224 | tf_op jit(solution)/shard_map/ppermute | solution.py:355
  74.3 1.6 %collective-permute-start.19 = (bf16[2,4,16,1024]{3,2,1,0:T(8,128)(2,1)S(1)}, bf16[2,4,16,1024]{3,2,1,0:T(8,128)(2,1)S(1)}, u32[]{:S(2)}, u32[]{:S(2)}) collective-permute-start(bf16[2,4,16,1024]{3,2,1,0:T(8,128)(2,1)S(1)} %get-tuple-element.70), channel_id=1, source_target_pairs={{0,8},{8,0},{16,24},{24,16},{1,9},{9,1},{17,25},{25,17},{2,10},{10... | collective-permute-start | bytes 786440 | tf_op jit(solution)/shard_map/ppermute | solution.py:482
where the time goes:
time: 77.7 us; the launch traced here: 76.9 us
  waiting for transfers between devices  36.9 us (47%)
  starting transfers between devices  25.1 us (32%)
  Pallas kernels  14 us (18%)
  between operations  0.81 us (1%)
    ppermute x8, starting transfers between devices, around(): lax.ppermute(part, ('ctx', 'enc'), [(i * n_enc + e, i * n_enc + (e ^ carr...  21 us
    ppermute x8, waiting for transfers between devices, around(): lax.ppermute(part, ('ctx', 'enc'), [(i * n_enc + e, i * n_enc + (e ^ carr...  13 us
    ppermute x2, waiting for transfers between devices, shards(): back[c] = lax.ppermute(grads, 'ctx', swap_y)  11.4 us
    pallas_call x12, Pallas kernels, call(): return local_call(body, [IN_VMEM] * len(args), spec, **more)(*args)  10.1 us
    ppermute x2, waiting for transfers between devices, shards(): far.append(lax.ppermute(own[-1], 'ctx', swap_y))  7.33 us
    ppermute x3, waiting for transfers between devices, shards(): lax.ppermute(for_peer, 'ctx', swap_core)  3.63 us
    ppermute x2, starting transfers between devices, shards(): far.append(lax.ppermute(own[-1], 'ctx', swap_y))  2.09 us
    pallas_call x1, Pallas kernels, shards(): local_call(split_kernel, [IN_HBM] * 6, [(slabs, BF16, IN_VMEM)] * 2 + tex...  2.04 us
  transfers between devices with their start and end apart: 20, of which 11 were waited for; matrix products, arithmetic and copies ran while one was open for 0% of the time, Pallas kernels for 11%

commit v1 on v0

--- a/solution.py
+++ b/solution.py
@@ -24,7 +24,6 @@
 CHUNK_KV = HALF_KV // CHUNKS
 CHUNK_KCOLS = CHUNK_KV * HD
 CHUNK_QCOLS = CHUNK_KV * WIDE
-BLOCKS = 4
 SAMP_ROWS = 16
 SCALE = HD ** (-0.5)
 LOG2E = 1.4426950408889634
@@ -89,31 +88,26 @@
     return [pltpu.with_memory_space_constraint(a, pltpu.HBM) for a in arrays]
 
 
-def carried(j, core):
-    return BLOCKS * (1 - core) + j
-
-
 def split_kernel(*refs):
     k_ref, v_ref, q_ref, g_ref, samp_hbm, tiles_hbm, mine, peer = refs[:8]
     text_refs, (samp, tiles, sems, small_sems) = refs[8:-4], refs[-4:]
     core = core_of()
-    enc = lax.axis_index("enc")
     pairs = []
-    for who, out in ((1 - core, peer), (core, mine)):
-        for j in range(BLOCKS):
+    for half, out in ((1 - core, peer), (core, mine)):
+        for c in range(CHUNKS):
+            cols = at_cols(half * HALF_KCOLS + c * CHUNK_KCOLS, CHUNK_KCOLS, CHUNK_KCOLS)
             for i, ref in enumerate((k_ref, v_ref)):
-                pairs.append((ref.at[enc ^ carried(j, who)], out.at[i, j]))
+                pairs.append((ref.at[:, :, cols], out.at[c, i]))
     copies = start_copies(pairs, sems)
     split_text(
-        2 * BLOCKS, CORES, near_place, q_ref, g_ref, samp_hbm, tiles_hbm, *text_refs, samp, tiles, small_sems
+        k_ref.shape[0], CORES, near_place, q_ref, g_ref, samp_hbm, tiles_hbm, *text_refs, samp, tiles, small_sems
     )
     for copy in copies:
         copy.wait()
 
 
 def near_place():
-    y = lax.div(lax.axis_index("ctx"), CORES)
-    return y, lax.axis_index("enc") ^ carried(0, core_of())
+    return lax.div(lax.axis_index("ctx"), CORES), lax.axis_index("enc")
 
 
 def split_text(n_blocks, pieces, where, q_ref, g_ref, samp_hbm, tiles_hbm, peer, q_own, g_own, bias, samp, tiles, sems):
@@ -139,11 +133,15 @@
         out[first:, :] = jnp.zeros((SAMP_ROWS, HALF_QCOLS), BF16)
         out[first:, :tokens] = row
 
-    sample, offset = where()
+    sample, enc = where()
     block_rows = SLOT_ROWS // n_blocks
     slots = block_rows // pieces
     line = lax.broadcasted_iota(jnp.int32, (SLOT_ROWS, HD), 0)
-    owner = lax.div(line, block_rows) ^ offset
+    block = lax.div(line, block_rows)
+    if n_blocks > 1:
+        n_z = n_blocks // 2
+        block = 2 * lax.rem(block, n_z) + lax.div(block, n_z)
+    owner = block ^ enc
     piece = lax.rem(lax.div(line, slots), pieces)
     slot = piece * (SLOT_ROWS // pieces) + owner * slots + lax.rem(line, slots)
     for i in range(SAMP):
@@ -153,68 +151,60 @@
         copy.wait()
 
 
-def carry_kernel(slots, mine, got, text, *outs):
-    core = core_of()
-    for j, out in enumerate(outs[:-1]):
-        for i in range(2):
-            first = i * CORES * slots
-            out[at_rows(first + core * slots, slots), :] = mine[i, j]
-            out[at_rows(first + (1 - core) * slots, slots), :] = got[i, j]
+def carry_kernel(slots, own, got, text, *outs):
+    core = core_of()
+    enc = lax.axis_index("enc")
+    n_z = (len(outs) - 1) // CHUNKS
+    for c in range(CHUNKS):
+        for dz in range(n_z):
+            out = outs[c * n_z + dz]
+            for dx in range(2):
+                group = enc ^ (2 * dz + dx)
+                for i in range(2):
+                    first = i * CORES * slots
+                    out[dx, at_rows(first + core * slots, slots), :] = own[c, i, group]
+                    out[dx, at_rows(first + (1 - core) * slots, slots), :] = got[c, i, group]
 
 
 def join_kernel(*refs):
-    parts, out = refs[:-1], refs[-1]
-    rows = parts[0].shape[0]
-    for i, part in enumerate(parts):
-        out[i * rows : (i + 1) * rows, :] = part[...]
-
-
-def split_cols_kernel(*refs):
-    parts, out = refs[: BLOCKS // 2], refs[-1]
-    rows = parts[0].shape[0]
-    cols = at_cols((1 - core_of()) * HALF_KCOLS, HALF_KCOLS, HALF_KCOLS)
-    for i, part in enumerate(parts):
-        out[i * rows : (i + 1) * rows, :] = part[:, cols]
-
-
-def add_kernel(*refs):
-    own, back, outs = refs[:CHUNKS], refs[CHUNKS : 2 * CHUNKS], refs[2 * CHUNKS :]
-    rows = outs[0].shape[0]
-    for i, out in enumerate(outs):
-        part = slice(i * rows, (i + 1) * rows)
+    parts, outs = refs[:-2], refs[-2:]
+    rows = parts[0].shape[1]
+    for dx, out in enumerate(outs):
+        for dz, part in enumerate(parts):
+            out[dz * rows : (dz + 1) * rows, :] = part[dx]
+
+
+def add_kernel(own, back_y, back_x, back_xy, *outs):
+    rows = outs[0].shape[1]
+    for dz, out in enumerate(outs):
+        part = slice(dz * rows, (dz + 1) * rows)
+        out[0] = (own[part, :] + back_y[part, :].astype(F32)).astype(out.dtype)
+        out[1] = (back_x[part, :].astype(F32) + back_xy[part, :].astype(F32)).astype(out.dtype)
+
+
+def owner_rows_kernel(slots, n_z, *refs):
+    core = core_of()
+    enc = lax.axis_index("enc")
+    parts, (mine_out, peer_out) = refs[: CHUNKS * n_z], refs[-2:]
+    for c in range(CHUNKS):
+        for dz in range(n_z):
+            part = parts[c * n_z + dz]
+            for dx in range(2):
+                group = enc ^ (2 * dz + dx)
+                for i in range(2):
+                    first = i * CORES * slots
+                    mine_out[c, i, group] = part[dx, at_rows(first + core * slots, slots), :]
+                    peer_out[c, i, group] = part[dx, at_rows(first + (1 - core) * slots, slots), :]
+
+
+def finish_kernel(mine, got, dk, dv, sems):
+    core = core_of()
+    pairs = []
+    for half, ref in ((core, mine), (1 - core, got)):
         for c in range(CHUNKS):
-            cols = slice(c * CHUNK_KCOLS, (c + 1) * CHUNK_KCOLS)
-            out[:, cols] = (own[c][part, :] + back[c][part, :].astype(F32)).astype(out.dtype)
-
-
-def back_kernel(mine, got, *outs):
-    core = core_of()
-    rows = outs[0].shape[0]
-    own_cols = at_cols(core * HALF_KCOLS, HALF_KCOLS, HALF_KCOLS)
-    got_cols = at_cols((1 - core) * HALF_KCOLS, HALF_KCOLS, HALF_KCOLS)
-    for j, out in enumerate(outs):
-        out[:, own_cols] = mine[j * rows : (j + 1) * rows, :]
-        out[:, got_cols] = got[j * rows : (j + 1) * rows, :]
-
-
-def owner_rows_kernel(slots, *refs):
-    blocks, (mine, peer) = refs[: BLOCKS], refs[-2:]
-    core = core_of()
-    for j, block in enumerate(blocks):
-        for i in range(2):
-            first = i * CORES * slots
-            mine[i, j] = block[at_rows(first + core * slots, slots), :]
-            peer[i, j] = block[at_rows(first + (1 - core) * slots, slots), :]
-
-
-def finish_kernel(mine, got, dk, dv, sems):
-    core = core_of()
-    enc = lax.axis_index("enc")
-    pairs = []
-    for who, ref in ((core, mine), (1 - core, got)):
-        for j in range(BLOCKS):
+            cols = at_cols(half * HALF_KCOLS + c * CHUNK_KCOLS, CHUNK_KCOLS, CHUNK_KCOLS)
             for i, out in enumerate((dk, dv)):
-                pairs.append((ref.at[i, j], out.at[enc ^ carried(j, who)]))
+                pairs.append((ref.at[c, i], out.at[:, :, cols]))
     run_copies(pairs, sems)
 
 
@@ -235,7 +225,7 @@
     prev = None
     if with_prev:
         prev, rest = rest[:2], rest[2:]
-    *dqs, grads = rest
+    dqs, grads = rest[:2], rest[2:]
     sample = where()[0] ^ role
     tokens = g_a.shape[0]
     block_rows = SLOT_ROWS // n_blocks
@@ -250,7 +240,6 @@
         mine = jnp.concatenate([row_a] * RATIO + [row_b] * RATIO, axis=1) == wanted
         for h in range(CHUNK_KV):
             first_q = chunk * CHUNK_QCOLS + h * WIDE
-            first_k = chunk * CHUNK_KCOLS + h * HD
 
             def stacked(ref_a, first_b):
                 parts = [
@@ -263,12 +252,8 @@
             def rows_of(first):
                 parts = []
                 for kv in kvs:
-                    if kv.shape[1] == HALF_KCOLS:
-                        cols = slice(first_k, first_k + HD)
-                    else:
-                        cols = at_cols(core_of() * HALF_KCOLS + first_k, HD, HD)
                     for at in range(first, kv.shape[0], 2 * block_rows):
-                        parts.append(kv[at : at + block_rows, cols])
+                        parts.append(kv[at : at + block_rows, h * HD : (h + 1) * HD])
                 return jnp.concatenate(parts, axis=0)
 
             q = stacked(q_a, 0)
@@ -296,28 +281,30 @@
                         part = part + prev[t][:, cols].astype(F32)
                     dq_ref[:, cols] = part.astype(dq_ref.dtype)
             cols = slice(h * HD, (h + 1) * HD)
+            each = n_blocks // len(grads)
             for b in range(n_blocks):
                 rows = slice(b * block_rows, (b + 1) * block_rows)
-                first = b * 2 * block_rows
-                grads[first : first + block_rows, cols] = dk[rows].astype(grads.dtype)
-                grads[first + block_rows : first + 2 * block_rows, cols] = dv[rows].astype(grads.dtype)
+                out, first = grads[b // each], b % each * 2 * block_rows
+                out[first : first + block_rows, cols] = dk[rows].astype(out.dtype)
+                out[first + block_rows : first + 2 * block_rows, cols] = dv[rows].astype(out.dtype)
 
     @pl.when(jnp.logical_not(present))
     def _():
-        grads[...] = jnp.zeros_like(grads)
+        for out in grads:
+            out[...] = jnp.zeros_like(out)
         for t, dq_ref in enumerate(dqs):
             dq_ref[...] = prev[t][...] if with_prev else jnp.zeros_like(dq_ref)
 
 
-def sample_pass(where, role, chunk, n_blocks, bias, text, kvs, prev, grad_dtype):
+def sample_pass(where, role, chunk, n_blocks, bias, text, kvs, prev, grad_dtypes):
     tokens = text[1].shape[0]
     dq = ((tokens, CHUNK_QCOLS), BF16)
     pairs = tokens * WIDE * SLOT_ROWS * CORES * CHUNK_KV
-    dq_a, dq_b, grads = in_vmem(
+    dq_a, dq_b, *grads = in_vmem(
         functools.partial(
             pass_kernel, role, chunk, n_blocks, len(kvs), prev is not None, where
         ),
-        [dq, dq, ((2 * SLOT_ROWS, CHUNK_KCOLS), grad_dtype)],
+        [dq, dq] + [(kv.shape, dtype) for kv, dtype in zip(kvs, grad_dtypes)],
         flops=10 * pairs,
         moved=8 * 2**20,
     )(bias, *text, *kvs, *(prev or ()))
@@ -329,7 +316,7 @@
     slots = img_k.shape[1]
     tokens = queries.shape[1]
     swap_core = [(i, i ^ 1) for i in range(n_ctx)]
-    near = n_y == SAMP and slots % 16 == 0 and n_enc == 2 * BLOCKS
+    near = n_y == SAMP and slots % 16 == 0 and n_enc == 8
     dqs = [None] * CHUNKS
     text_outs = [
         ((2 * tokens + SAMP_ROWS, HALF_QCOLS), BF16, IN_VMEM),
@@ -345,66 +332,64 @@
 
     if near:
         swap_y = [(i, (i + CORES) % n_ctx) for i in range(n_ctx)]
-        block = (2 * CORES * slots, KVH * HD)
-        pair = (2 * block[0], block[1])
-        half = (BLOCKS * block[0], HALF_KCOLS)
-        slabs = (2, BLOCKS, slots, KVH * HD)
-
-        def around(parts):
-            return [
-                lax.ppermute(
-                    part,
-                    ("ctx", "enc"),
-                    [
-                        (i * n_enc + e, i * n_enc + (e ^ carried(j, i % CORES)))
-                        for i in range(n_ctx)
-                        for e in range(n_enc)
-                    ],
-                )
-                for j, part in enumerate(parts)
+        n_z = n_enc // 2
+        pair = (2, 2 * CORES * slots, CHUNK_KCOLS)
+        half = (SLOT_ROWS, CHUNK_KCOLS)
+        halves = (CHUNKS, 2, n_enc, slots, CHUNK_KCOLS)
+        swap_x = [(i, i ^ 1) for i in range(n_enc)]
+        swap_xy = [
+            (i * n_enc + e, (i + CORES) % n_ctx * n_enc + (e ^ 1))
+            for i in range(n_ctx)
+            for e in range(n_enc)
+        ]
+
+        def around_z(parts):
+            moved = [
+                lax.ppermute(parts[dz], "enc", [(i, i ^ (2 * dz)) for i in range(n_enc)])
+                for dz in range(1, n_z)
             ]
+            return [parts[0], *moved]
+
+        def along_x(part):
+            return lax.ppermute(part, "enc", swap_x)
+
+        def along_y(part):
+            return lax.ppermute(part, "ctx", swap_y)
+
+        def along_xy(part):
+            return lax.ppermute(part, ("ctx", "enc"), swap_xy)
 
         mine, for_peer, text_peer, q_own, g_own, bias = local_call(
             split_kernel,
             [IN_HBM] * 6,
-            [(slabs, BF16, IN_VMEM)] * 2 + text_outs,
-            text_scratch + [pltpu.SemaphoreType.DMA((4 * BLOCKS,)), text_sems],
+            [(halves, BF16, IN_VMEM)] * 2 + text_outs,
+            text_scratch + [pltpu.SemaphoreType.DMA((4 * CHUNKS,)), text_sems],
             moved=4 * 2**20,
         )(*in_hbm(img_k, img_v, queries, d_out, text_sample, tiles))
         *carry, text_peer = in_vmem(
             functools.partial(carry_kernel, slots),
-            [(block, BF16)] * BLOCKS + [(text_peer.shape, BF16)],
-            aliases={2: BLOCKS},
+            [(pair, BF16)] * CHUNKS * n_z + [(text_peer.shape, BF16)],
+            aliases={2: CHUNKS * n_z},
         )(mine, lax.ppermute(for_peer, "ctx", swap_core), text_peer)
         text = (q_own, g_own, lax.ppermute(text_peer, "ctx", swap_core))
-        brought = around(carry)
-
-        def with_other_core(parts, after=()):
-            (for_peer,) = in_vmem(split_cols_kernel, [(half, BF16)])(*parts, *after)
-            return [*parts, lax.ppermute(for_peer, "ctx", swap_core)]
-
-        own, far = [], []
-        for j in range(0, BLOCKS, 2):
-            own += in_vmem(join_kernel, [(pair, BF16)])(*brought[j : j + 2])
-            far.append(lax.ppermute(own[-1], "ctx", swap_y))
-        own = with_other_core(own)
-
-        own_grads, back = [None] * CHUNKS, [None] * CHUNKS
+
+        returned = []
         for c in range(CHUNKS):
-            dqs[c], own_grads[c] = sample_pass(
-                near_place, 0, c, n_enc, bias, text, own, None, F32
+            came = around_z(carry[c * n_z : (c + 1) * n_z])
+            here, beside = in_vmem(join_kernel, [(half, BF16)] * 2)(*came)
+            own = [here, along_x(beside)]
+            far = [along_y(here), along_xy(beside)]
+            dqs[c], (own_here, own_beside) = sample_pass(
+                near_place, 0, c, n_enc, bias, text, own, None, (F32, BF16)
             )
-        far = with_other_core(far, [pair[0] for pair in dqs])
-        for c in range(CHUNKS):
-            dqs[c], grads = sample_pass(
-                near_place, 1, c, n_enc, bias, text, far, dqs[c], BF16
+            back_x = along_x(own_beside)
+            dqs[c], (far_here, far_beside) = sample_pass(
+                near_place, 1, c, n_enc, bias, text, far, dqs[c], (BF16, BF16)
             )
-            back[c] = lax.ppermute(grads, "ctx", swap_y)
-        mine, for_peer = in_vmem(add_kernel, [(half, BF16)] * 2)(*own_grads, *back)
-        carry = in_vmem(back_kernel, [(block, BF16)] * BLOCKS)(
-            mine, lax.ppermute(for_peer, "ctx", swap_core)
-        )
-        brought = around(carry)
+            totals = in_vmem(add_kernel, [(pair, BF16)] * n_z)(
+                own_here, along_y(far_here), back_x, along_xy(far_beside)
+            )
+            returned += around_z(totals)
     else:
         both = ("ctx", "enc")
         same_y = [
@@ -454,8 +439,9 @@
         for sample in range(SAMP):
             rows = slice(sample * SLOT_ROWS, (sample + 1) * SLOT_ROWS)
             kv = jnp.concatenate([all_k[rows], all_v[rows]], axis=0)
+            kv = jnp.split(kv, CHUNKS, axis=1)
             for c in range(CHUNKS):
-                dqs[c], grads = sample_pass(no_place, sample, c, 1, bias, text, [kv], dqs[c], BF16)
+                dqs[c], (grads,) = sample_pass(no_place, sample, c, 1, bias, text, [kv[c]], dqs[c], (BF16,))
                 dks[sample][c] = grads[:SLOT_ROWS]
                 dvs[sample][c] = grads[SLOT_ROWS:]
         d_img_k = to_owners(jnp.block(dks))
@@ -472,13 +458,13 @@
     )(*ends)
     if near:
         mine, for_peer = in_vmem(
-            functools.partial(owner_rows_kernel, slots), [(slabs, BF16)] * 2
-        )(*brought, token)
+            functools.partial(owner_rows_kernel, slots, n_z), [(halves, BF16)] * 2
+        )(*returned, token)
         d_img_k, d_img_v = local_call(
             finish_kernel,
             [IN_VMEM] * 2,
             [(img_k.shape, BF16, IN_HBM)] * 2,
-            [pltpu.SemaphoreType.DMA((4 * BLOCKS,))],
+            [pltpu.SemaphoreType.DMA((4 * CHUNKS,))],
         )(mine, lax.ppermute(for_peer, "ctx", swap_core))
     return (d_queries, d_img_k, d_img_v)
 

time: 77.7 us -> 66.6 us (0.86)
  waiting for transfers between devices: 36.9 us -> 14.8 us
  starting transfers between devices: 25.1 us -> 37.1 us
    ppermute x14 -> x24, waiting for transfers between devices: 33.3 us -> 12.1 us  [the longest x12 7.37 us: around_z(): lax.ppermute(parts[dz], 'enc', [(i, i ^ 2 * dz) for i in range(n_enc)])]
    ppermute x14 -> x24, starting transfers between devices: 23.4 us -> 35.5 us  [the longest x12 20.7 us: around_z(): lax.ppermute(parts[dz], 'enc', [(i, i ^ 2 * dz) for i in range(n_enc)])]
    ppermute x3 -> x2, waiting for transfers between devices: 3.63 us -> 2.68 us  [shards(): lax.ppermute(for_peer, 'ctx', swap_core)]
    pallas_call x12 -> x10, Pallas kernels: 10.1 us -> 9.96 us  [call(): return local_call(body, [IN_VMEM] * len(args), spec, **more)(*args)]
  transfers between devices with their start and end apart: 20 -> 29, of which waited for: 11 -> 9; matrix products, arithmetic and copies ran while one was open for 0% -> 0% of each run, Pallas kernels for 11% -> 16%
where the time goes in v1:
time: 66.6 us; the launch traced here: 66.5 us
  starting transfers between devices  37.1 us (56%)
  waiting for transfers between devices  14.8 us (22%)
  Pallas kernels  13.7 us (21%)
  between operations  0.81 us (1%)
    ppermute x12, starting transfers between devices, around_z(): lax.ppermute(parts[dz], 'enc', [(i, i ^ 2 * dz) for i in range(n_enc)])  20.7 us
    pallas_call x10, Pallas kernels, call(): return local_call(body, [IN_VMEM] * len(args), spec, **more)(*args)  9.96 us
    ppermute x12, waiting for transfers between devices, around_z(): lax.ppermute(parts[dz], 'enc', [(i, i ^ 2 * dz) for i in range(n_enc)])  7.37 us
    ppermute x4, starting transfers between devices, along_xy(): return lax.ppermute(part, ('ctx', 'enc'), swap_xy)  6.63 us
    ppermute x4, starting transfers between devices, along_x(): return lax.ppermute(part, 'enc', swap_x)  5.97 us
    ppermute x4, waiting for transfers between devices, along_y(): return lax.ppermute(part, 'ctx', swap_y)  4.75 us
    ppermute x2, waiting for transfers between devices, shards(): lax.ppermute(for_peer, 'ctx', swap_core)  2.68 us
    ppermute x4, starting transfers between devices, along_y(): return lax.ppermute(part, 'ctx', swap_y)  2.1 us
  transfers between devices with their start and end apart: 29, of which 9 were waited for; matrix products, arithmetic and copies ran while one was open for 0% of the time, Pallas kernels for 16%

profile of v1, /device:TPU:0, one launch (start us, length us, event | category | flops | bytes accessed | tf_op | source)
XLA Modules:
  0.0 66.5 jit_solution(7051751437330685470)
XLA Ops:
  0.6 1.9 %shard_map.85 = (bf16[2,2,8,16,256]{4,3,2,1,0:T(8,128)(2,1)S(1)}, bf16[2,2,8,16,256]{4,3,2,1,0:T(8,128)(2,1)S(1)}, bf16[272,2048]{1,0:T(8,128)(2,1)S(1)}, bf16[1...) custom-call(bf16[8,16,1024]{2,1,0:T(8,128)(2,1)} %refs_0_.1, ...), custom_call_target="tpu_custom_call" | custom-call | bytes 4194304 | tf_op jit(solution)/shard_map/pallas_call | solution.py:362
  2.6 0.5 collective-permute-start
  3.1 1.2 %collective-permute-done.got = bf16[2,2,8,16,256]{4,3,2,1,0:T(8,128)(2,1)S(1)} collective-permute-done((bf16[2,2,8,16,256]{4,3,2,1,0:T(8,128)(2,1)S(1)}, bf16[2,2,8,16,256]{4,3,2,1,0:T(8,128)(2,1)S(1)}, u32[]{:S(2)}, u32[]{:S(2)}) %collective-permute-start) | collective-permute-done | bytes 262176 | tf_op jit(solution)/shard_map/ppermute | solution.py:373
  4.3 0.4 collective-permute-start.1
  4.7 2.7 %collective-permute-start.9 = (bf16[2,64,256]{2,1,0:T(8,128)(2,1)S(1)}, bf16[2,64,256]{2,1,0:T(8,128)(2,1)S(1)}, u32[]{:S(2)}, u32[]{:S(2)}) collective-permute-start(bf16[2,64,256]{2,1,0:T(8,128)(2,1)S(1)} %get-tuple-element.70), channel_id=1, source_target_pairs={{0,2},{1,3},{2,0},{3,1},{4,6},{5,7},{6,4},{7,5},{8,10},{9,11},{10,... | collective-permute-start | bytes 196616 | tf_op jit(solution)/shard_map/ppermute | solution.py:348
  7.5 2.6 %collective-permute-start.10 = (bf16[2,64,256]{2,1,0:T(8,128)(2,1)S(1)}, bf16[2,64,256]{2,1,0:T(8,128)(2,1)S(1)}, u32[]{:S(2)}, u32[]{:S(2)}) collective-permute-start(bf16[2,64,256]{2,1,0:T(8,128)(2,1)S(1)} %get-tuple-element.71), channel_id=1, source_target_pairs={{0,4},{1,5},{2,6},{3,7},{4,0},{5,1},{6,2},{7,3},{8,12},{9,13},{10,... | collective-permute-start | bytes 196616 | tf_op jit(solution)/shard_map/ppermute | solution.py:348
  10.1 0.9 %collective-permute-start.2 = (bf16[2,64,256]{2,1,0:T(8,128)(2,1)S(1)}, bf16[2,64,256]{2,1,0:T(8,128)(2,1)S(1)}, u32[]{:S(2)}, u32[]{:S(2)}) collective-permute-start(bf16[2,64,256]{2,1,0:T(8,128)(2,1)S(1)} %get-tuple-element.60), channel_id=1, source_target_pairs={{0,2},{1,3},{2,0},{3,1},{4,6},{5,7},{6,4},{7,5},{8,10},{9,11},{10,... | collective-permute-start | bytes 196616 | tf_op jit(solution)/shard_map/ppermute | solution.py:348
  10.9 0.0 collective-permute-done.9.refs_1_
  11.0 3.5 %collective-permute-start.3 = (bf16[2,64,256]{2,1,0:T(8,128)(2,1)S(1)}, bf16[2,64,256]{2,1,0:T(8,128)(2,1)S(1)}, u32[]{:S(2)}, u32[]{:S(2)}) collective-permute-start(bf16[2,64,256]{2,1,0:T(8,128)(2,1)S(1)} %get-tuple-element.61), channel_id=1, source_target_pairs={{0,4},{1,5},{2,6},{3,7},{4,0},{5,1},{6,2},{7,3},{8,12},{9,13},{10,... | collective-permute-start | bytes 196616 | tf_op jit(solution)/shard_map/ppermute | solution.py:348
  14.4 0.7 %collective-permute-done.10.refs_2_ = bf16[2,64,256]{2,1,0:T(8,128)(2,1)S(1)} collective-permute-done((bf16[2,64,256]{2,1,0:T(8,128)(2,1)S(1)}, bf16[2,64,256]{2,1,0:T(8,128)(2,1)S(1)}, u32[]{:S(2)}, u32[]{:S(2)}) %collective-permute-start.10) | collective-permute-done | bytes 65568 | tf_op jit(solution)/shard_map/ppermute | solution.py:348
  15.1 1.7 %collective-permute-done.11.refs_3_ = bf16[2,64,256]{2,1,0:T(8,128)(2,1)S(1)} collective-permute-done((bf16[2,64,256]{2,1,0:T(8,128)(2,1)S(1)}, bf16[2,64,256]{2,1,0:T(8,128)(2,1)S(1)}, u32[]{:S(2)}, u32[]{:S(2)}) %collective-permute-start.11) | collective-permute-done | bytes 65568 | tf_op jit(solution)/shard_map/ppermute | solution.py:348
  16.9 1.6 %collective-permute-start.14 = (bf16[256,256]{1,0:T(8,128)(2,1)S(1)}, bf16[256,256]{1,0:T(8,128)(2,1)S(1)}, u32[]{:S(2)}, u32[]{:S(2)}) collective-permute-start(bf16[256,256]{1,0:T(8,128)(2,1)S(1)} %get-tuple-element.74), channel_id=1, source_target_pairs={{0,1},{1,0},{2,3},{3,2},{4,5},{5,4},{6,7},{7,6},{8,9},{9,8},{10,11... | collective-permute-start | bytes 393224 | tf_op jit(solution)/shard_map/ppermute | solution.py:354
  18.4 2.2 %collective-permute-start.4 = (bf16[2,64,256]{2,1,0:T(8,128)(2,1)S(1)}, bf16[2,64,256]{2,1,0:T(8,128)(2,1)S(1)}, u32[]{:S(2)}, u32[]{:S(2)}) collective-permute-start(bf16[2,64,256]{2,1,0:T(8,128)(2,1)S(1)} %get-tuple-element.62), channel_id=1, source_target_pairs={{0,6},{1,7},{2,4},{3,5},{4,2},{5,3},{6,0},{7,1},{8,14},{9,15},{10,... | collective-permute-start | bytes 196616 | tf_op jit(solution)/shard_map/ppermute | solution.py:348
  20.6 0.0 collective-permute-done.2.refs_1_
  20.6 1.5 %collective-permute-start.12 = (bf16[256,256]{1,0:T(8,128)(2,1)S(1)}, bf16[256,256]{1,0:T(8,128)(2,1)S(1)}, u32[]{:S(2)}, u32[]{:S(2)}) collective-permute-start(bf16[256,256]{1,0:T(8,128)(2,1)S(1)} %get-tuple-element.73.rest_0_), channel_id=1, source_target_pairs={{0,16},{8,24},{16,0},{24,8},{1,17},{9,25},{17,1},{25,9},{2,18},{10... | collective-permute-start | bytes 393224 | tf_op jit(solution)/shard_map/ppermute | solution.py:357
  22.2 1.0 %collective-permute-start.13 = (bf16[256,256]{1,0:T(8,128)(2,1)S(1)}, bf16[256,256]{1,0:T(8,128)(2,1)S(1)}, u32[]{:S(2)}, u32[]{:S(2)}) collective-permute-start(bf16[256,256]{1,0:T(8,128)(2,1)S(1)} %get-tuple-element.74), channel_id=1, source_target_pairs={{0,17},{1,16},{2,19},{3,18},{4,21},{5,20},{6,23},{7,22},{8,25},{9,... | collective-permute-start | bytes 393224 | tf_op jit(solution)/shard_map/ppermute | solution.py:360
  23.2 1.3 %collective-permute-done.4.refs_3_ = bf16[2,64,256]{2,1,0:T(8,128)(2,1)S(1)} collective-permute-done((bf16[2,64,256]{2,1,0:T(8,128)(2,1)S(1)}, bf16[2,64,256]{2,1,0:T(8,128)(2,1)S(1)}, u32[]{:S(2)}, u32[]{:S(2)}) %collective-permute-start.4) | collective-permute-done | bytes 65568 | tf_op jit(solution)/shard_map/ppermute | solution.py:348
  24.5 0.6 collective-permute-start.7
  25.2 2.4 %collective-permute-start.6 = (bf16[256,256]{1,0:T(8,128)(2,1)S(1)}, bf16[256,256]{1,0:T(8,128)(2,1)S(1)}, u32[]{:S(2)}, u32[]{:S(2)}) collective-permute-start(bf16[256,256]{1,0:T(8,128)(2,1)S(1)} %get-tuple-element.64), channel_id=1, source_target_pairs={{0,17},{1,16},{2,19},{3,18},{4,21},{5,20},{6,23},{7,22},{8,25},{9,... | collective-permute-start | bytes 393224 | tf_op jit(solution)/shard_map/ppermute | solution.py:360
  27.6 0.0 collective-permute-done.1.got
  27.6 0.5 collective-permute-start.5
  28.1 2.4 %shard_map.91 = (bf16[128,1024]{1,0:T(8,128)(2,1)S(1)}, bf16[128,1024]{1,0:T(8,128)(2,1)S(1)}, f32[256,256]{1,0:T(8,128)S(1)}, bf16[256,256]{1,0:T(8,128)(2,1)S(1)}) custom-call(f32[2,256,128]{2,1,0:T(8,128)S(1)} %get-tuple-element.52.bias, bf16[144,2048]{1,0:T(8,128)(2,1)S(1)} %get-tuple-element.53.q_a, bf16[128,2048]{1,0:T(8,128)(2,1)S(1)} %get-tuple-element.54.g_a, ...), custom_call_target="tpu_custom_call" | custom-call | flops 671088640 | bytes 8388608 | tf_op jit(solution)/shard_map/pallas_call | solution.py:58
  30.5 2.4 %shard_map.92 = (bf16[128,1024]{1,0:T(8,128)(2,1)S(1)}, bf16[128,1024]{1,0:T(8,128)(2,1)S(1)}, bf16[256,256]{1,0:T(8,128)(2,1)S(1)}, bf16[256,256]{1,0:T(8,128)(2,1)S(1)}) custom-call(f32[2,256,128]{2,1,0:T(8,128)S(1)} %get-tuple-element.52.bias, bf16[144,2048]{1,0:T(8,128)(2,1)S(1)} %get-tuple-element.53.q_a, bf16[128,2048]{1,0:T(8,128)(2,1)S(1)} %get-tuple-element.54.g_a, ...), custom_call_target="tpu_custom_call" | custom-call | flops 671088640 | bytes 8388608 | tf_op jit(solution)/shard_map/pallas_call | solution.py:58
  33.0 0.1 collective-permute-start.22
  33.1 1.6 %collective-permute-start.24 = (bf16[256,256]{1,0:T(8,128)(2,1)S(1)}, bf16[256,256]{1,0:T(8,128)(2,1)S(1)}, u32[]{:S(2)}, u32[]{:S(2)}) collective-permute-start(bf16[256,256]{1,0:T(8,128)(2,1)S(1)} %get-tuple-element.91), channel_id=1, source_target_pairs={{0,17},{1,16},{2,19},{3,18},{4,21},{5,20},{6,23},{7,22},{8,25},{9,... | collective-permute-start | bytes 393224 | tf_op jit(solution)/shard_map/ppermute | solution.py:360
  34.7 1.9 %collective-permute-start.23 = (bf16[256,256]{1,0:T(8,128)(2,1)S(1)}, bf16[256,256]{1,0:T(8,128)(2,1)S(1)}, u32[]{:S(2)}, u32[]{:S(2)}) collective-permute-start(bf16[256,256]{1,0:T(8,128)(2,1)S(1)} %get-tuple-element.90), channel_id=1, source_target_pairs={{0,1},{1,0},{2,3},{3,2},{4,5},{5,4},{6,7},{7,6},{8,9},{9,8},{10,11... | collective-permute-start | bytes 393224 | tf_op jit(solution)/shard_map/ppermute | solution.py:354
  36.6 2.4 %shard_map.88 = (bf16[128,1024]{1,0:T(8,128)(2,1)S(1)}, bf16[128,1024]{1,0:T(8,128)(2,1)S(1)}, f32[256,256]{1,0:T(8,128)S(1)}, bf16[256,256]{1,0:T(8,128)(2,1)S(1)}) custom-call(f32[2,256,128]{2,1,0:T(8,128)S(1)} %get-tuple-element.52.bias, bf16[144,2048]{1,0:T(8,128)(2,1)S(1)} %get-tuple-element.53.q_a, bf16[128,2048]{1,0:T(8,128)(2,1)S(1)} %get-tuple-element.54.g_a, ...), custom_call_target="tpu_custom_call" | custom-call | flops 671088640 | bytes 8388608 | tf_op jit(solution)/shard_map/pallas_call | solution.py:58
  39.0 0.1 collective-permute-start.15
  39.1 2.4 %shard_map.89 = (bf16[128,1024]{1,0:T(8,128)(2,1)S(1)}, bf16[128,1024]{1,0:T(8,128)(2,1)S(1)}, bf16[256,256]{1,0:T(8,128)(2,1)S(1)}, bf16[256,256]{1,0:T(8,128)(2,1)S(1)}) custom-call(f32[2,256,128]{2,1,0:T(8,128)S(1)} %get-tuple-element.52.bias, bf16[144,2048]{1,0:T(8,128)(2,1)S(1)} %get-tuple-element.53.q_a, bf16[128,2048]{1,0:T(8,128)(2,1)S(1)} %get-tuple-element.54.g_a, ...), custom_call_target="tpu_custom_call" | custom-call | flops 671088640 | bytes 8388608 | tf_op jit(solution)/shard_map/pallas_call | solution.py:58
  41.5 0.5 collective-permute-start.8
  42.1 1.6 %collective-permute-start.18 = (bf16[256,256]{1,0:T(8,128)(2,1)S(1)}, bf16[256,256]{1,0:T(8,128)(2,1)S(1)}, u32[]{:S(2)}, u32[]{:S(2)}) collective-permute-start(bf16[256,256]{1,0:T(8,128)(2,1)S(1)} %get-tuple-element.83), channel_id=1, source_target_pairs={{0,17},{1,16},{2,19},{3,18},{4,21},{5,20},{6,23},{7,22},{8,25},{9,... | collective-permute-start | bytes 393224 | tf_op jit(solution)/shard_map/ppermute | solution.py:360
  43.7 1.9 %collective-permute-start.17 = (bf16[256,256]{1,0:T(8,128)(2,1)S(1)}, bf16[256,256]{1,0:T(8,128)(2,1)S(1)}, u32[]{:S(2)}, u32[]{:S(2)}) collective-permute-start(bf16[256,256]{1,0:T(8,128)(2,1)S(1)} %get-tuple-element.82), channel_id=1, source_target_pairs={{0,1},{1,0},{2,3},{3,2},{4,5},{5,4},{6,7},{7,6},{8,9},{9,8},{10,11... | collective-permute-start | bytes 393224 | tf_op jit(solution)/shard_map/ppermute | solution.py:354
  45.6 0.1 shard_map.95
  45.6 4.7 %collective-permute-done.16.back_y = bf16[256,256]{1,0:T(8,128)(2,1)S(1)} collective-permute-done((bf16[256,256]{1,0:T(8,128)(2,1)S(1)}, bf16[256,256]{1,0:T(8,128)(2,1)S(1)}, u32[]{:S(2)}, u32[]{:S(2)}) %collective-permute-start.16) | collective-permute-done | bytes 131104 | tf_op jit(solution)/shard_map/ppermute | solution.py:357
  50.4 0.3 collective-permute-start.25
  50.6 2.6 %collective-permute-start.26 = (bf16[2,64,256]{2,1,0:T(8,128)(2,1)S(1)}, bf16[2,64,256]{2,1,0:T(8,128)(2,1)S(1)}, u32[]{:S(2)}, u32[]{:S(2)}) collective-permute-start(bf16[2,64,256]{2,1,0:T(8,128)(2,1)S(1)} %get-tuple-element.94), channel_id=1, source_target_pairs={{0,4},{1,5},{2,6},{3,7},{4,0},{5,1},{6,2},{7,3},{8,12},{9,13},{10,... | collective-permute-start | bytes 196616 | tf_op jit(solution)/shard_map/ppermute | solution.py:348
  53.3 1.5 %collective-permute-start.27 = (bf16[2,64,256]{2,1,0:T(8,128)(2,1)S(1)}, bf16[2,64,256]{2,1,0:T(8,128)(2,1)S(1)}, u32[]{:S(2)}, u32[]{:S(2)}) collective-permute-start(bf16[2,64,256]{2,1,0:T(8,128)(2,1)S(1)} %get-tuple-element.95), channel_id=1, source_target_pairs={{0,6},{1,7},{2,4},{3,5},{4,2},{5,3},{6,0},{7,1},{8,14},{9,15},{10,... | collective-permute-start | bytes 196616 | tf_op jit(solution)/shard_map/ppermute | solution.py:348
  54.8 0.1 shard_map.94
  54.8 0.2 collective-permute-start.19
  55.1 2.7 %collective-permute-start.20 = (bf16[2,64,256]{2,1,0:T(8,128)(2,1)S(1)}, bf16[2,64,256]{2,1,0:T(8,128)(2,1)S(1)}, u32[]{:S(2)}, u32[]{:S(2)}) collective-permute-start(bf16[2,64,256]{2,1,0:T(8,128)(2,1)S(1)} %get-tuple-element.86), channel_id=1, source_target_pairs={{0,4},{1,5},{2,6},{3,7},{4,0},{5,1},{6,2},{7,3},{8,12},{9,13},{10,... | collective-permute-start | bytes 196616 | tf_op jit(solution)/shard_map/ppermute | solution.py:348
  57.8 1.5 %collective-permute-start.21 = (bf16[2,64,256]{2,1,0:T(8,128)(2,1)S(1)}, bf16[2,64,256]{2,1,0:T(8,128)(2,1)S(1)}, u32[]{:S(2)}, u32[]{:S(2)}) collective-permute-start(bf16[2,64,256]{2,1,0:T(8,128)(2,1)S(1)} %get-tuple-element.87), channel_id=1, source_target_pairs={{0,6},{1,7},{2,4},{3,5},{4,2},{5,3},{6,0},{7,1},{8,14},{9,15},{10,... | collective-permute-start | bytes 196616 | tf_op jit(solution)/shard_map/ppermute | solution.py:348
  59.3 1.0 %shard_map.93 = (bf16[1,128,4096]{2,1,0:T(8,128)(2,1)}, f32[8,128]{1,0:T(8,128)S(1)}) custom-call(bf16[128,1024]{1,0:T(8,128)(2,1)S(1)} %get-tuple-element.67.refs_0_, bf16[128,1024]{1,0:T(8,128)(2,1)S(1)} %collective-permute-done.8.refs_1_, bf16[128,1024]{1,0:T(8,128)(2,1)S(1)} %get-tuple-element.77.refs_2_, ...), custom_call_target="tpu_custom_call" | custom-call | bytes 524288 | tf_op jit(solution)/shard_map/pallas_call | solution.py:453
  60.3 0.7 collective-permute-done.19.refs_1_
  61.0 2.2 %collective-permute-done.20.refs_2_ = bf16[2,64,256]{2,1,0:T(8,128)(2,1)S(1)} collective-permute-done((bf16[2,64,256]{2,1,0:T(8,128)(2,1)S(1)}, bf16[2,64,256]{2,1,0:T(8,128)(2,1)S(1)}, u32[]{:S(2)}, u32[]{:S(2)}) %collective-permute-start.20) | collective-permute-done | bytes 65568 | tf_op jit(solution)/shard_map/ppermute | solution.py:348
  63.2 0.7 %collective-permute-done.21.refs_3_ = bf16[2,64,256]{2,1,0:T(8,128)(2,1)S(1)} collective-permute-done((bf16[2,64,256]{2,1,0:T(8,128)(2,1)S(1)}, bf16[2,64,256]{2,1,0:T(8,128)(2,1)S(1)}, u32[]{:S(2)}, u32[]{:S(2)}) %collective-permute-start.21) | collective-permute-done | bytes 65568 | tf_op jit(solution)/shard_map/ppermute | solution.py:348
  64.0 0.1 collective-permute-start.28
  64.1 1.5 %collective-permute-done.28.got = bf16[2,2,8,16,256]{4,3,2,1,0:T(8,128)(2,1)S(1)} collective-permute-done((bf16[2,2,8,16,256]{4,3,2,1,0:T(8,128)(2,1)S(1)}, bf16[2,2,8,16,256]{4,3,2,1,0:T(8,128)(2,1)S(1)}, u32[]{:S(2)}, u32[]{:S(2)}) %collective-permute-start.28) | collective-permute-done | bytes 262176 | tf_op jit(solution)/shard_map/ppermute | solution.py:468
  65.6 0.8 %shard_map.97 = (bf16[8,16,1024]{2,1,0:T(8,128)(2,1)}, bf16[8,16,1024]{2,1,0:T(8,128)(2,1)}) custom-call(bf16[2,2,8,16,256]{4,3,2,1,0:T(8,128)(2,1)S(1)} %get-tuple-element.97.mine, bf16[2,2,8,16,256]{4,3,2,1,0:T(8,128)(2,1)S(1)} %collective-permute-done.28.got), custom_call_target="tpu_custom_call" | custom-call | bytes 524288 | tf_op jit(solution)/shard_map/pallas_call | solution.py:463
  (23 shorter events, 0.2 us)
Async XLA Ops:
  2.6 1.7 %collective-permute-start = (bf16[2,2,8,16,256]{4,3,2,1,0:T(8,128)(2,1)S(1)}, bf16[2,2,8,16,256]{4,3,2,1,0:T(8,128)(2,1)S(1)}, u32[]{:S(2)}, u32[]{:S(2)}) collective-permute-start(bf16[2,2,8,16,256]{4,3,2,1,0:T(8,128)(2,1)S(1)} %get-tuple-element.56), channel_id=1, source_target_pairs={{0,8},{8,0},{16,24},{24,16},{1,9},{9,1},{17,25},{25,17},{2,10},{10... | collective-permute-start | bytes 786440 | tf_op jit(solution)/shard_map/ppermute | solution.py:373
  4.3 23.3 %collective-permute-start.1 = (bf16[272,2048]{1,0:T(8,128)(2,1)S(1)}, bf16[272,2048]{1,0:T(8,128)(2,1)S(1)}, u32[]{:S(2)}, u32[]{:S(2)}) collective-permute-start(bf16[272,2048]{1,0:T(8,128)(2,1)S(1)} %get-tuple-element.58), channel_id=1, source_target_pairs={{0,8},{8,0},{16,24},{24,16},{1,9},{9,1},{17,25},{25,17},{2,10},{10... | collective-permute-start | bytes 3342344 | tf_op jit(solution)/shard_map/ppermute | solution.py:374
  4.7 6.2 %collective-permute-start.9 = (bf16[2,64,256]{2,1,0:T(8,128)(2,1)S(1)}, bf16[2,64,256]{2,1,0:T(8,128)(2,1)S(1)}, u32[]{:S(2)}, u32[]{:S(2)}) collective-permute-start(bf16[2,64,256]{2,1,0:T(8,128)(2,1)S(1)} %get-tuple-element.70), channel_id=1, source_target_pairs={{0,2},{1,3},{2,0},{3,1},{4,6},{5,7},{6,4},{7,5},{8,10},{9,11},{10,... | collective-permute-start | bytes 196616 | tf_op jit(solution)/shard_map/ppermute | solution.py:348
  7.5 7.7 %collective-permute-start.10 = (bf16[2,64,256]{2,1,0:T(8,128)(2,1)S(1)}, bf16[2,64,256]{2,1,0:T(8,128)(2,1)S(1)}, u32[]{:S(2)}, u32[]{:S(2)}) collective-permute-start(bf16[2,64,256]{2,1,0:T(8,128)(2,1)S(1)} %get-tuple-element.71), channel_id=1, source_target_pairs={{0,4},{1,5},{2,6},{3,7},{4,0},{5,1},{6,2},{7,3},{8,12},{9,13},{10,... | collective-permute-start | bytes 196616 | tf_op jit(solution)/shard_map/ppermute | solution.py:348
  10.0 6.8 %collective-permute-start.11 = (bf16[2,64,256]{2,1,0:T(8,128)(2,1)S(1)}, bf16[2,64,256]{2,1,0:T(8,128)(2,1)S(1)}, u32[]{:S(2)}, u32[]{:S(2)}) collective-permute-start(bf16[2,64,256]{2,1,0:T(8,128)(2,1)S(1)} %get-tuple-element.72), channel_id=1, source_target_pairs={{0,6},{1,7},{2,4},{3,5},{4,2},{5,3},{6,0},{7,1},{8,14},{9,15},{10,... | collective-permute-start | bytes 196616 | tf_op jit(solution)/shard_map/ppermute | solution.py:348
  10.1 10.6 %collective-permute-start.2 = (bf16[2,64,256]{2,1,0:T(8,128)(2,1)S(1)}, bf16[2,64,256]{2,1,0:T(8,128)(2,1)S(1)}, u32[]{:S(2)}, u32[]{:S(2)}) collective-permute-start(bf16[2,64,256]{2,1,0:T(8,128)(2,1)S(1)} %get-tuple-element.60), channel_id=1, source_target_pairs={{0,2},{1,3},{2,0},{3,1},{4,6},{5,7},{6,4},{7,5},{8,10},{9,11},{10,... | collective-permute-start | bytes 196616 | tf_op jit(solution)/shard_map/ppermute | solution.py:348
  11.0 11.2 %collective-permute-start.3 = (bf16[2,64,256]{2,1,0:T(8,128)(2,1)S(1)}, bf16[2,64,256]{2,1,0:T(8,128)(2,1)S(1)}, u32[]{:S(2)}, u32[]{:S(2)}) collective-permute-start(bf16[2,64,256]{2,1,0:T(8,128)(2,1)S(1)} %get-tuple-element.61), channel_id=1, source_target_pairs={{0,4},{1,5},{2,6},{3,7},{4,0},{5,1},{6,2},{7,3},{8,12},{9,13},{10,... | collective-permute-start | bytes 196616 | tf_op jit(solution)/shard_map/ppermute | solution.py:348
  16.9 8.3 %collective-permute-start.14 = (bf16[256,256]{1,0:T(8,128)(2,1)S(1)}, bf16[256,256]{1,0:T(8,128)(2,1)S(1)}, u32[]{:S(2)}, u32[]{:S(2)}) collective-permute-start(bf16[256,256]{1,0:T(8,128)(2,1)S(1)} %get-tuple-element.74), channel_id=1, source_target_pairs={{0,1},{1,0},{2,3},{3,2},{4,5},{5,4},{6,7},{7,6},{8,9},{9,8},{10,11... | collective-permute-start | bytes 393224 | tf_op jit(solution)/shard_map/ppermute | solution.py:354
  18.4 6.1 %collective-permute-start.4 = (bf16[2,64,256]{2,1,0:T(8,128)(2,1)S(1)}, bf16[2,64,256]{2,1,0:T(8,128)(2,1)S(1)}, u32[]{:S(2)}, u32[]{:S(2)}) collective-permute-start(bf16[2,64,256]{2,1,0:T(8,128)(2,1)S(1)} %get-tuple-element.62), channel_id=1, source_target_pairs={{0,6},{1,7},{2,4},{3,5},{4,2},{5,3},{6,0},{7,1},{8,14},{9,15},{10,... | collective-permute-start | bytes 196616 | tf_op jit(solution)/shard_map/ppermute | solution.py:348
  20.6 9.9 %collective-permute-start.12 = (bf16[256,256]{1,0:T(8,128)(2,1)S(1)}, bf16[256,256]{1,0:T(8,128)(2,1)S(1)}, u32[]{:S(2)}, u32[]{:S(2)}) collective-permute-start(bf16[256,256]{1,0:T(8,128)(2,1)S(1)} %get-tuple-element.73.rest_0_), channel_id=1, source_target_pairs={{0,16},{8,24},{16,0},{24,8},{1,17},{9,25},{17,1},{25,9},{2,18},{10... | collective-permute-start | bytes 393224 | tf_op jit(solution)/shard_map/ppermute | solution.py:357
  22.2 8.4 %collective-permute-start.13 = (bf16[256,256]{1,0:T(8,128)(2,1)S(1)}, bf16[256,256]{1,0:T(8,128)(2,1)S(1)}, u32[]{:S(2)}, u32[]{:S(2)}) collective-permute-start(bf16[256,256]{1,0:T(8,128)(2,1)S(1)} %get-tuple-element.74), channel_id=1, source_target_pairs={{0,17},{1,16},{2,19},{3,18},{4,21},{5,20},{6,23},{7,22},{8,25},{9,... | collective-permute-start | bytes 393224 | tf_op jit(solution)/shard_map/ppermute | solution.py:360
  24.5 10.1 %collective-permute-start.7 = (bf16[256,256]{1,0:T(8,128)(2,1)S(1)}, bf16[256,256]{1,0:T(8,128)(2,1)S(1)}, u32[]{:S(2)}, u32[]{:S(2)}) collective-permute-start(bf16[256,256]{1,0:T(8,128)(2,1)S(1)} %get-tuple-element.64), channel_id=1, source_target_pairs={{0,1},{1,0},{2,3},{3,2},{4,5},{5,4},{6,7},{7,6},{8,9},{9,8},{10,11... | collective-permute-start | bytes 393224 | tf_op jit(solution)/shard_map/ppermute | solution.py:354
  25.2 13.9 %collective-permute-start.6 = (bf16[256,256]{1,0:T(8,128)(2,1)S(1)}, bf16[256,256]{1,0:T(8,128)(2,1)S(1)}, u32[]{:S(2)}, u32[]{:S(2)}) collective-permute-start(bf16[256,256]{1,0:T(8,128)(2,1)S(1)} %get-tuple-element.64), channel_id=1, source_target_pairs={{0,17},{1,16},{2,19},{3,18},{4,21},{5,20},{6,23},{7,22},{8,25},{9,... | collective-permute-start | bytes 393224 | tf_op jit(solution)/shard_map/ppermute | solution.py:360
  27.6 11.4 %collective-permute-start.5 = (bf16[256,256]{1,0:T(8,128)(2,1)S(1)}, bf16[256,256]{1,0:T(8,128)(2,1)S(1)}, u32[]{:S(2)}, u32[]{:S(2)}) collective-permute-start(bf16[256,256]{1,0:T(8,128)(2,1)S(1)} %get-tuple-element.63.rest_0_), channel_id=1, source_target_pairs={{0,16},{8,24},{16,0},{24,8},{1,17},{9,25},{17,1},{25,9},{2,18},{10... | collective-permute-start | bytes 393224 | tf_op jit(solution)/shard_map/ppermute | solution.py:357
  33.0 9.1 %collective-permute-start.22 = (bf16[256,256]{1,0:T(8,128)(2,1)S(1)}, bf16[256,256]{1,0:T(8,128)(2,1)S(1)}, u32[]{:S(2)}, u32[]{:S(2)}) collective-permute-start(bf16[256,256]{1,0:T(8,128)(2,1)S(1)} %get-tuple-element.89), channel_id=1, source_target_pairs={{0,16},{8,24},{16,0},{24,8},{1,17},{9,25},{17,1},{25,9},{2,18},{10... | collective-permute-start | bytes 393224 | tf_op jit(solution)/shard_map/ppermute | solution.py:357
  33.1 9.0 %collective-permute-start.24 = (bf16[256,256]{1,0:T(8,128)(2,1)S(1)}, bf16[256,256]{1,0:T(8,128)(2,1)S(1)}, u32[]{:S(2)}, u32[]{:S(2)}) collective-permute-start(bf16[256,256]{1,0:T(8,128)(2,1)S(1)} %get-tuple-element.91), channel_id=1, source_target_pairs={{0,17},{1,16},{2,19},{3,18},{4,21},{5,20},{6,23},{7,22},{8,25},{9,... | collective-permute-start | bytes 393224 | tf_op jit(solution)/shard_map/ppermute | solution.py:360
  34.7 9.0 %collective-permute-start.23 = (bf16[256,256]{1,0:T(8,128)(2,1)S(1)}, bf16[256,256]{1,0:T(8,128)(2,1)S(1)}, u32[]{:S(2)}, u32[]{:S(2)}) collective-permute-start(bf16[256,256]{1,0:T(8,128)(2,1)S(1)} %get-tuple-element.90), channel_id=1, source_target_pairs={{0,1},{1,0},{2,3},{3,2},{4,5},{5,4},{6,7},{7,6},{8,9},{9,8},{10,11... | collective-permute-start | bytes 393224 | tf_op jit(solution)/shard_map/ppermute | solution.py:354
  39.0 16.1 %collective-permute-start.15 = (bf16[128,1024]{1,0:T(8,128)(2,1)S(1)}, bf16[128,1024]{1,0:T(8,128)(2,1)S(1)}, u32[]{:S(2)}, u32[]{:S(2)}) collective-permute-start(bf16[128,1024]{1,0:T(8,128)(2,1)S(1)} %get-tuple-element.78), channel_id=1, source_target_pairs={{0,8},{8,0},{16,24},{24,16},{1,9},{9,1},{17,25},{25,17},{2,10},{10... | collective-permute-start | bytes 786440 | tf_op jit(solution)/shard_map/ppermute | solution.py:452
  41.5 16.3 %collective-permute-start.8 = (bf16[128,1024]{1,0:T(8,128)(2,1)S(1)}, bf16[128,1024]{1,0:T(8,128)(2,1)S(1)}, u32[]{:S(2)}, u32[]{:S(2)}) collective-permute-start(bf16[128,1024]{1,0:T(8,128)(2,1)S(1)} %get-tuple-element.68), channel_id=1, source_target_pairs={{0,8},{8,0},{16,24},{24,16},{1,9},{9,1},{17,25},{25,17},{2,10},{10... | collective-permute-start | bytes 786440 | tf_op jit(solution)/shard_map/ppermute | solution.py:452
  42.1 8.3 %collective-permute-start.16 = (bf16[256,256]{1,0:T(8,128)(2,1)S(1)}, bf16[256,256]{1,0:T(8,128)(2,1)S(1)}, u32[]{:S(2)}, u32[]{:S(2)}) collective-permute-start(bf16[256,256]{1,0:T(8,128)(2,1)S(1)} %get-tuple-element.81), channel_id=1, source_target_pairs={{0,16},{8,24},{16,0},{24,8},{1,17},{9,25},{17,1},{25,9},{2,18},{10... | collective-permute-start | bytes 393224 | tf_op jit(solution)/shard_map/ppermute | solution.py:357
  42.1 8.6 %collective-permute-start.18 = (bf16[256,256]{1,0:T(8,128)(2,1)S(1)}, bf16[256,256]{1,0:T(8,128)(2,1)S(1)}, u32[]{:S(2)}, u32[]{:S(2)}) collective-permute-start(bf16[256,256]{1,0:T(8,128)(2,1)S(1)} %get-tuple-element.83), channel_id=1, source_target_pairs={{0,17},{1,16},{2,19},{3,18},{4,21},{5,20},{6,23},{7,22},{8,25},{9,... | collective-permute-start | bytes 393224 | tf_op jit(solution)/shard_map/ppermute | solution.py:360
  43.7 9.6 %collective-permute-start.17 = (bf16[256,256]{1,0:T(8,128)(2,1)S(1)}, bf16[256,256]{1,0:T(8,128)(2,1)S(1)}, u32[]{:S(2)}, u32[]{:S(2)}) collective-permute-start(bf16[256,256]{1,0:T(8,128)(2,1)S(1)} %get-tuple-element.82), channel_id=1, source_target_pairs={{0,1},{1,0},{2,3},{3,2},{4,5},{5,4},{6,7},{7,6},{8,9},{9,8},{10,11... | collective-permute-start | bytes 393224 | tf_op jit(solution)/shard_map/ppermute | solution.py:354
  50.4 4.5 %collective-permute-start.25 = (bf16[2,64,256]{2,1,0:T(8,128)(2,1)S(1)}, bf16[2,64,256]{2,1,0:T(8,128)(2,1)S(1)}, u32[]{:S(2)}, u32[]{:S(2)}) collective-permute-start(bf16[2,64,256]{2,1,0:T(8,128)(2,1)S(1)} %get-tuple-element.93), channel_id=1, source_target_pairs={{0,2},{1,3},{2,0},{3,1},{4,6},{5,7},{6,4},{7,5},{8,10},{9,11},{10,... | collective-permute-start | bytes 196616 | tf_op jit(solution)/shard_map/ppermute | solution.py:348
  50.6 9.7 %collective-permute-start.26 = (bf16[2,64,256]{2,1,0:T(8,128)(2,1)S(1)}, bf16[2,64,256]{2,1,0:T(8,128)(2,1)S(1)}, u32[]{:S(2)}, u32[]{:S(2)}) collective-permute-start(bf16[2,64,256]{2,1,0:T(8,128)(2,1)S(1)} %get-tuple-element.94), channel_id=1, source_target_pairs={{0,4},{1,5},{2,6},{3,7},{4,0},{5,1},{6,2},{7,3},{8,12},{9,13},{10,... | collective-permute-start | bytes 196616 | tf_op jit(solution)/shard_map/ppermute | solution.py:348
  53.3 7.1 %collective-permute-start.27 = (bf16[2,64,256]{2,1,0:T(8,128)(2,1)S(1)}, bf16[2,64,256]{2,1,0:T(8,128)(2,1)S(1)}, u32[]{:S(2)}, u32[]{:S(2)}) collective-permute-start(bf16[2,64,256]{2,1,0:T(8,128)(2,1)S(1)} %get-tuple-element.95), channel_id=1, source_target_pairs={{0,6},{1,7},{2,4},{3,5},{4,2},{5,3},{6,0},{7,1},{8,14},{9,15},{10,... | collective-permute-start | bytes 196616 | tf_op jit(solution)/shard_map/ppermute | solution.py:348
  54.8 6.1 %collective-permute-start.19 = (bf16[2,64,256]{2,1,0:T(8,128)(2,1)S(1)}, bf16[2,64,256]{2,1,0:T(8,128)(2,1)S(1)}, u32[]{:S(2)}, u32[]{:S(2)}) collective-permute-start(bf16[2,64,256]{2,1,0:T(8,128)(2,1)S(1)} %get-tuple-element.85), channel_id=1, source_target_pairs={{0,2},{1,3},{2,0},{3,1},{4,6},{5,7},{6,4},{7,5},{8,10},{9,11},{10,... | collective-permute-start | bytes 196616 | tf_op jit(solution)/shard_map/ppermute | solution.py:348
  55.1 8.1 %collective-permute-start.20 = (bf16[2,64,256]{2,1,0:T(8,128)(2,1)S(1)}, bf16[2,64,256]{2,1,0:T(8,128)(2,1)S(1)}, u32[]{:S(2)}, u32[]{:S(2)}) collective-permute-start(bf16[2,64,256]{2,1,0:T(8,128)(2,1)S(1)} %get-tuple-element.86), channel_id=1, source_target_pairs={{0,4},{1,5},{2,6},{3,7},{4,0},{5,1},{6,2},{7,3},{8,12},{9,13},{10,... | collective-permute-start | bytes 196616 | tf_op jit(solution)/shard_map/ppermute | solution.py:348
  57.8 6.2 %collective-permute-start.21 = (bf16[2,64,256]{2,1,0:T(8,128)(2,1)S(1)}, bf16[2,64,256]{2,1,0:T(8,128)(2,1)S(1)}, u32[]{:S(2)}, u32[]{:S(2)}) collective-permute-start(bf16[2,64,256]{2,1,0:T(8,128)(2,1)S(1)} %get-tuple-element.87), channel_id=1, source_target_pairs={{0,6},{1,7},{2,4},{3,5},{4,2},{5,3},{6,0},{7,1},{8,14},{9,15},{10,... | collective-permute-start | bytes 196616 | tf_op jit(solution)/shard_map/ppermute | solution.py:348
  64.0 1.6 %collective-permute-start.28 = (bf16[2,2,8,16,256]{4,3,2,1,0:T(8,128)(2,1)S(1)}, bf16[2,2,8,16,256]{4,3,2,1,0:T(8,128)(2,1)S(1)}, u32[]{:S(2)}, u32[]{:S(2)}) collective-permute-start(bf16[2,2,8,16,256]{4,3,2,1,0:T(8,128)(2,1)S(1)} %get-tuple-element.98), channel_id=1, source_target_pairs={{0,8},{8,0},{16,24},{24,16},{1,9},{9,1},{17,25},{25,17},{2,10},{10... | collective-permute-start | bytes 786440 | tf_op jit(solution)/shard_map/ppermute | solution.py:468
